TPU v7x, 128 devices: a whole 4x4x4 slice. The times are simulated.
128 devices in a mesh: node: 8 (over z, core), local: 16 (over y, x).
Axes of the slice: x: 4, y: 4, z: 4, core: 2. Of those that a mesh axis runs over, the one named last changes fastest.
Arguments:
- tokens: bfloat16 [16384, 3584], P(('node', 'local')), may hold values from -6 to 6
- expert_ids: int32 [16384, 8], P(('node', 'local')), may hold values from 0 to 127, as said below
- combine_weights: bfloat16 [16384, 8], P(('node', 'local')), may hold values from 0.049804688 to 0.59765625
- gate_weight: bfloat16 [128, 3584, 1024], P(('node', 'local')), may hold values from -0.09375 to 0.09375
- up_weight: bfloat16 [128, 3584, 1024], P(('node', 'local')), may hold values from -0.09375 to 0.09375
- down_weight: bfloat16 [128, 1024, 3584], P(('node', 'local')), may hold values from -0.1875 to 0.1875
- latent_rows: bfloat16 [16384, 576], P(('node', 'local')), may hold values from -6 to 6
- latent_owner: int32 [16384], P(('node', 'local')), may hold values from 0 to 127, as said below
Outputs:
- moe_out: bfloat16 [16384, 3584], P(('node', 'local'))
- latent_cache: bfloat16 [16384, 576], P(('node', 'local'))
Inputs may be any that keep to these rules, and one draw needn't show every extreme that they name: `expert_ids`: each token names 8 different experts, 2 on each of exactly 4 different nodes, where expert e lies on node e // 16. Of the tokens of one device, exactly 64 reach each node. Among the tokens of all devices that share one local index and reach one node, each expert of that node is named at most 80 times, and some experts are named exactly 80 times. `latent_owner`: devices are numbered node-major. Each device sends either no rows or exactly 2 rows to each owner, and each owner receives exactly 128 rows.
All inputs are finite; a program needn't handle non-finite values.
Results may differ from a plain program's by a relative error of at most 0.0064.
Values may be sent and summed in bfloat16 or wider, within the bound.
A program may use at most 128 MiB of HBM per device.

v0:
```python
import jax
import jax.numpy as jnp
from jax import lax
from jax.sharding import PartitionSpec as P

NODES_MAX = 4
LAT_CAP = 2
PER_NODE = 2


def expert_block(rows_in, gate_weight, up_weight, down_weight):
    senders, slot_count, row_width = rows_in.shape
    flat_in = rows_in.reshape(senders * slot_count, row_width)
    gate_act = jnp.dot(flat_in, gate_weight[0], preferred_element_type=jnp.float32)
    up_act = jnp.dot(flat_in, up_weight[0], preferred_element_type=jnp.float32)
    hidden = (jax.nn.silu(gate_act) * up_act).astype(jnp.bfloat16)
    result = jnp.dot(hidden, down_weight[0], preferred_element_type=jnp.float32).astype(
        jnp.bfloat16
    )
    return result.reshape(senders, slot_count, row_width)


def per_device(
    tokens,
    expert_ids,
    combine_weights,
    gate_weight,
    up_weight,
    down_weight,
    latent_rows,
    latent_owner,
):
    node_count = lax.axis_size("node")
    local_count = lax.axis_size("local")
    tok_count, row_width = tokens.shape
    top_count = expert_ids.shape[1]
    node_slots = tok_count * NODES_MAX // node_count
    capacity = 5 * top_count * tok_count // (4 * local_count)
    expert_range = jnp.arange(node_count * local_count, dtype=jnp.int32)
    hit_table = expert_ids[:, :, None] == expert_range[None, None, :]
    gate_table = jnp.sum(
        jnp.where(hit_table, combine_weights[:, :, None].astype(jnp.float32), 0.0), axis=1
    )
    gate_table = gate_table.reshape(tok_count, node_count, local_count)
    hit_grid = jnp.any(hit_table, axis=1).reshape(tok_count, node_count, local_count)
    picked = jnp.any(hit_grid, axis=2)
    node_rank = jnp.cumsum(picked.astype(jnp.int32), axis=0) - 1
    slot_range = jnp.arange(node_slots, dtype=jnp.int32)
    choose = picked.T[:, None, :] & (node_rank.T[:, None, :] == slot_range[None, :, None])
    choose_bf = choose.astype(jnp.bfloat16)
    send_rows = jnp.einsum(
        "nst,td->nsd", choose_bf, tokens, preferred_element_type=jnp.float32
    ).astype(jnp.bfloat16)
    send_gates = jnp.einsum(
        "nst,tnl->nsl", choose.astype(jnp.float32), gate_table, precision=lax.Precision.HIGHEST
    ).astype(jnp.bfloat16)
    got_rows, got_gates = (
        lax.all_to_all(send_rows, "node", split_axis=0, concat_axis=0, tiled=True),
        lax.all_to_all(send_gates, "node", split_axis=0, concat_axis=0, tiled=True),
    )
    rows_total = node_count * node_slots
    flat_rows = got_rows.reshape(rows_total, row_width)
    flat_gates = got_gates.reshape(rows_total, local_count).astype(jnp.float32)
    routed = flat_gates > 0
    expert_slot = jnp.cumsum(routed.astype(jnp.int32), axis=0) - 1
    cap_range = jnp.arange(capacity, dtype=jnp.int32)
    placed = routed.T[:, None, :] & (expert_slot.T[:, None, :] == cap_range[None, :, None])
    row_range = jnp.arange(rows_total, dtype=jnp.int32)
    source_row = jnp.sum(jnp.where(placed, row_range[None, None, :], 0), axis=2)
    filled = jnp.any(placed, axis=2)
    outgoing = jnp.where(filled[:, :, None], flat_rows[source_row], jnp.zeros((), jnp.bfloat16))
    produced = expert_block(
        lax.all_to_all(outgoing, "local", split_axis=0, concat_axis=0, tiled=True),
        gate_weight,
        up_weight,
        down_weight,
    )
    returned = lax.all_to_all(produced, "local", split_axis=0, concat_axis=0, tiled=True)
    order_in_row = jnp.cumsum(routed.astype(jnp.int32), axis=1) - 1
    pair_range = jnp.arange(PER_NODE, dtype=jnp.int32)
    local_range = jnp.arange(local_count, dtype=jnp.int32)
    pair_mask = routed[:, None, :] & (order_in_row[:, None, :] == pair_range[None, :, None])
    local_pick = jnp.sum(jnp.where(pair_mask, local_range[None, None, :], 0), axis=2)
    slot_pick = jnp.take_along_axis(expert_slot, local_pick, axis=1)
    pair_rows = returned[local_pick, slot_pick].reshape(
        node_count, node_slots * PER_NODE, row_width
    )
    home_pairs = lax.all_to_all(pair_rows, "node", split_axis=0, concat_axis=0, tiled=True)
    home_pairs = home_pairs.reshape(node_count, node_slots, PER_NODE, row_width)
    sent_gates = send_gates.astype(jnp.float32)
    sent_routed = sent_gates > 0
    sent_order = jnp.cumsum(sent_routed.astype(jnp.int32), axis=2) - 1
    sent_mask = sent_routed[:, :, None, :] & (
        sent_order[:, :, None, :] == pair_range[None, None, :, None]
    )
    pair_gate = jnp.sum(jnp.where(sent_mask, sent_gates[:, :, None, :], 0.0), axis=3)
    partial_value = jnp.sum(pair_gate[:, :, :, None] * home_pairs.astype(jnp.float32), axis=2)
    home_rows = partial_value.astype(jnp.bfloat16)
    summed = jnp.einsum("nst,nsd->td", choose_bf, home_rows, preferred_element_type=jnp.float32)
    moe_out = summed.astype(jnp.bfloat16)
    lat_count = latent_rows.shape[0]
    device_count = node_count * local_count
    owner_hits = latent_owner[None, :] == jnp.arange(device_count, dtype=jnp.int32)[:, None]
    owner_slot = jnp.cumsum(owner_hits.astype(jnp.int32), axis=1) - 1
    lat_range = jnp.arange(LAT_CAP, dtype=jnp.int32)
    lat_place = owner_hits[:, None, :] & (owner_slot[:, None, :] == lat_range[None, :, None])
    lat_send = jnp.einsum(
        "dcr,rk->dck",
        lat_place.astype(jnp.bfloat16),
        latent_rows,
        preferred_element_type=jnp.float32,
    ).astype(jnp.bfloat16)
    lat_mark = jnp.any(lat_place, axis=2).astype(jnp.bfloat16)
    lat_got, mark_got = (
        lax.all_to_all(lat_send, ("node", "local"), split_axis=0, concat_axis=0, tiled=True),
        lax.all_to_all(lat_mark, ("node", "local"), split_axis=0, concat_axis=0, tiled=True),
    )
    lat_flat = lat_got.reshape(device_count * LAT_CAP, -1)
    live_rows = mark_got.reshape(-1) > 0
    position = jnp.cumsum(live_rows.astype(jnp.int32)) - 1
    settle = live_rows[None, :] & (
        position[None, :] == jnp.arange(lat_count, dtype=jnp.int32)[:, None]
    )
    latent_cache = jnp.einsum(
        "jr,rk->jk", settle.astype(jnp.bfloat16), lat_flat, preferred_element_type=jnp.float32
    ).astype(jnp.bfloat16)
    return (moe_out, latent_cache)


def solution(mesh):
    in_specs = (
        P(("node", "local"), None),
        P(("node", "local"), None),
        P(("node", "local"), None),
        P(("node", "local"), None, None),
        P(("node", "local"), None, None),
        P(("node", "local"), None, None),
        P(("node", "local"), None),
        P(("node", "local")),
    )
    out_specs = (P(("node", "local"), None), P(("node", "local"), None))
    return jax.shard_map(
        per_device, mesh=mesh, in_specs=in_specs, out_specs=out_specs, check_vma=False
    )
```

profile of v0, /device:TPU:1, one launch (start us, length us, event | category | flops | bytes accessed | tf_op | source)
XLA Modules:
  0.0 610.1 jit_solution(15154702849827647983)
XLA Ops:
  0.6 0.9 copy.78
  1.5 0.3 fusion.12
  1.8 0.1 copy.79
  2.0 0.1 copy.80
  2.1 0.2 reduce_window_sum.74
  2.3 0.8 copy.82
  3.1 0.3 select_reduce_fusion.1
  3.4 0.1 copy.83
  3.5 1.0 fusion.40
  4.5 0.7 reshape.282
  5.2 6.8 %all-to-all-start = ((bf16[8,2,512]{2,1,0:T(2,128)(2,1)}), bf16[8,2,512]{2,1,0:T(2,128)(2,1)S(1)}, u32[]{:S(2)}, u32[]{:S(2)}) async-start(bf16[8,2,512]{2,1,0:T(2,128)(2,1)} %reshape.282), calls=%async_computation | async-start | bytes 32768 | tf_op jit(solution)/shard_map/all_to_all | solution.py:59
  12.0 2.9 convolution_convert_fusion.1
  14.9 1.8 all-to-all-done
  16.7 5.1 all-to-all-start.1
  21.8 0.1 reshape.283
  21.9 0.1 gt.39
  22.0 1.2 reduce-window.15
  23.2 0.2 slice_reduce_fusion
  23.5 0.7 select_reduce_fusion
  24.3 0.5 fusion.10
  24.8 40.3 %all-to-all-done.1 = bf16[8,64,3584]{2,1,0:T(8,128)(2,1)} async-done(((bf16[8,64,3584]{2,1,0:T(8,128)(2,1)}), bf16[8,64,3584]{2,1,0:T(8,128)(2,1)}, u32[]{:S(2)}, u32[]{:S(2)}) %all-to-all-start.1) | async-done | bytes 3670048 | tf_op jit(solution)/shard_map/all_to_all | solution.py:58
  65.1 19.7 %gather_fusion = bf16[1280,3584]{1,0:T(8,128)(2,1)} fusion(bf16[512,3584]{1,0:T(8,128)(2,1)} %bitcast.7, s32[2048]{0:T(1024)S(1)} %pad_clamp_fusion), kind=kCustom, calls=%fused_computation | custom fusion | bytes 18355200 | tf_op jit(solution)/shard_map/gather | solution.py:71
  84.8 7.9 %broadcast_select_fusion = bf16[16,80,3584]{2,1,0:T(8,128)(2,1)} fusion(bf16[16,80,3584]{2,1,0:T(8,128)(2,1)} %bitcast.77, pred[16,80]{1,0:T(8,128)(4,1)S(1)} %fusion.10), kind=kLoop, calls=%fused_computation.5 | loop fusion | flops 4587520 | bytes 18351360 | tf_op jit(solution)/shard_map/jit(_where)/select_n | solution.py:71
  92.6 6.9 %all-to-all-start.2 = ((bf16[16,80,3584]{2,1,0:T(8,128)(2,1)}), bf16[16,80,3584]{2,1,0:T(8,128)(2,1)}, u32[]{:S(2)}, u32[]{:S(2)}) async-start(bf16[16,80,3584]{2,1,0:T(8,128)(2,1)} %broadcast_select_fusion), calls=%async_computation.2 | async-start | bytes 18350080 | tf_op jit(solution)/shard_map/all_to_all | solution.py:73
  99.7 0.2 reduce_window_sum.78
  99.9 0.1 copy.94
  100.0 0.1 copy.93
  100.1 0.1 fusion.24
  100.2 0.8 copy.95
  101.0 132.7 %all-to-all-done.2 = bf16[16,80,3584]{2,1,0:T(8,128)(2,1)} async-done(((bf16[16,80,3584]{2,1,0:T(8,128)(2,1)}), bf16[16,80,3584]{2,1,0:T(8,128)(2,1)}, u32[]{:S(2)}, u32[]{:S(2)}) %all-to-all-start.2) | async-done | bytes 9175072 | tf_op jit(solution)/shard_map/all_to_all | solution.py:73
  233.7 8.0 %all-to-all-start.5 = ((bf16[128,1,2]{2,1,0:T(2,128)(2,1)}), bf16[128,1,2]{2,1,0:T(2,128)(2,1)S(1)}, u32[]{:S(2)}, u32[]{:S(2)}) async-start(bf16[128,1,2]{2,1,0:T(2,128)(2,1)} %copy.95), calls=%async_computation.5 | async-start | bytes 131072 | tf_op jit(solution)/shard_map/all_to_all | solution.py:116
  241.7 13.3 %fusion.1 = f32[1280,1024]{1,0:T(8,128)S(1)} fusion(bf16[1280,3584]{1,0:T(8,128)(2,1)} %bitcast.10, bf16[1,3584,1024]{2,1,0:T(8,128)(2,1)} %param.12), kind=kOutput, calls=%fused_computation.7 | convolution fusion | flops 9395240960 | bytes 21757952 | tf_op jit(solution)/shard_map/dot_general | solution.py:15
  255.0 14.9 %multiply_convert_fusion = bf16[1280,1024]{1,0:T(8,128)(2,1)S(1)} fusion(f32[1280,1024]{1,0:T(8,128)S(1)} %fusion.1, bf16[1280,3584]{1,0:T(8,128)(2,1)} %bitcast.10, bf16[1,3584,1024]{2,1,0:T(8,128)(2,1)} %param.11), kind=kOutput, calls=%fused_computation.12 | convolution fusion | flops 9403105280 | bytes 24379392 | tf_op jit(solution)/shard_map/dot_general | solution.py:14
  269.9 14.9 %convolution_convert_fusion = bf16[1280,3584]{1,0:T(8,128)(2,1)} fusion(bf16[1280,1024]{1,0:T(8,128)(2,1)S(1)} %multiply_convert_fusion, bf16[1,1024,3584]{2,1,0:T(8,128)(2,1)} %param.13), kind=kOutput, calls=%fused_computation.3 | convolution fusion | flops 9399828480 | bytes 19136512 | tf_op jit(solution)/shard_map/dot_general | solution.py:17
  284.8 6.9 %all-to-all-start.3 = ((bf16[16,80,3584]{2,1,0:T(8,128)(2,1)}), bf16[16,80,3584]{2,1,0:T(8,128)(2,1)}, u32[]{:S(2)}, u32[]{:S(2)}) async-start(bf16[16,80,3584]{2,1,0:T(8,128)(2,1)} %bitcast.79), calls=%async_computation.3 | async-start | bytes 18350080 | tf_op jit(solution)/shard_map/all_to_all | solution.py:78
  291.7 0.2 convolution_convert_fusion.2
  291.9 1.3 copy.96
  293.3 134.7 %all-to-all-done.3 = bf16[16,80,3584]{2,1,0:T(8,128)(2,1)} async-done(((bf16[16,80,3584]{2,1,0:T(8,128)(2,1)}), bf16[16,80,3584]{2,1,0:T(8,128)(2,1)}, u32[]{:S(2)}, u32[]{:S(2)}) %all-to-all-start.3) | async-done | bytes 9175072 | tf_op jit(solution)/shard_map/all_to_all | solution.py:78
  428.0 8.4 %all-to-all-start.6 = ((bf16[128,2,576]{2,1,0:T(2,128)(2,1)}), bf16[128,2,576]{2,1,0:T(2,128)(2,1)S(1)}, u32[]{:S(2)}, u32[]{:S(2)}) async-start(bf16[128,2,576]{2,1,0:T(2,128)(2,1)} %copy.96), calls=%async_computation.6 | async-start | bytes 655360 | tf_op jit(solution)/shard_map/all_to_all | solution.py:115
  436.4 0.1 copy.90
  436.6 0.2 reshape.260
  436.8 8.6 %gather_fusion.2 = s32[1024]{0:T(1024)S(1)} fusion(s32[512,16]{0,1:T(8,128)S(1)} %get-tuple-element.4, s32[1024]{0:T(1024)S(1)} %reshape.260), kind=kCustom, calls=%fused_computation.2 | custom fusion | bytes 16384 | tf_op jit(solution)/shard_map/jit(take_along_axis)/gather | solution.py:84
  445.4 0.2 gather.14
  445.6 0.1 copy.91
  445.8 0.1 copy.92
  445.9 0.2 reshape.254
  446.1 32.2 %gather_fusion.1 = bf16[1024,3584]{1,0:T(8,128)(2,1)} fusion(bf16[16,80,3584]{2,1,0:T(8,128)(2,1)} %all-to-all-done.3, s32[1024]{0:T(1024)S(1)} %reshape.254), kind=kCustom, calls=%fused_computation.1 | custom fusion | bytes 14688256 | tf_op jit(solution)/shard_map/gather | solution.py:85
  478.3 6.1 all-to-all-start.4
  484.3 0.1 copy.84
  484.5 1.5 reduce_window_sum.75
  486.0 0.1 copy.85
  486.2 0.2 copy.86
  486.3 0.2 fusion.30
  486.6 0.1 reshape.245
  486.7 0.3 reduce-window.19
  487.1 0.2 compare_reduce_fusion
  487.4 0.1 gt.42
  487.5 0.1 slice_reduce_fusion.1
  487.7 0.3 reshape.242
  488.0 1.0 convolution_convert_fusion.3
  488.9 78.0 %all-to-all-done.4 = bf16[8,128,3584]{2,1,0:T(8,128)(2,1)} async-done(((bf16[8,128,3584]{2,1,0:T(8,128)(2,1)}), bf16[8,128,3584]{2,1,0:T(8,128)(2,1)}, u32[]{:S(2)}, u32[]{:S(2)}) %all-to-all-start.4) | async-done | bytes 7340064 | tf_op jit(solution)/shard_map/all_to_all | solution.py:88
  567.0 16.3 %reshape.243 = f32[8,64,2,3584]{3,2,1,0:T(2,128)} reshape(bf16[8,128,3584]{2,1,0:T(8,128)(2,1)} %all-to-all-done.4) | data formatting | bytes 22020096 | tf_op jit(solution)/shard_map/convert_element_type | solution.py:97
  583.2 23.2 %multiply_reduce_fusion = bf16[8,64,3584]{2,1,0:T(8,128)(2,1)} fusion(f32[8,64,2,3584]{3,2,1,0:T(2,128)} %reshape.243, f32[8,64,2]{2,1,0:T(8,128)S(1)} %copy.86), kind=kLoop, calls=%fused_computation.4 | loop fusion | flops 5505024 | bytes 18354176 | tf_op jit(solution)/shard_map/reduce_sum | solution.py:97
  606.4 3.7 fusion.7
  (52 shorter events, 0.9 us)
Async XLA Ops:
  0.6 11.4 %copy-start = (bf16[128,3584]{1,0:T(8,128)(2,1)S(1)}, bf16[128,3584]{1,0:T(8,128)(2,1)}, u32[]{:S(2)}) copy-start(bf16[128,3584]{1,0:T(8,128)(2,1)} %param.8) | copy-start | bytes 2752516
  1.9 82.8 %copy-start.8 = (pred[128,8]{0,1:T(8,128)(4,1)}, pred[128,8]{0,1:T(8,128)(4,1)S(1)}, u32[]{:S(2)}) copy-start(pred[128,8]{0,1:T(8,128)(4,1)S(1)} %bitcast_reduce_fusion) | copy-start | bytes 3076
  2.3 82.5 %copy-start.6 = (s32[8,128]{1,0:T(8,128)}, s32[8,128]{1,0:T(8,128)S(1)}, u32[]{:S(2)}) copy-start(s32[8,128]{1,0:T(8,128)S(1)} %copy.81) | copy-start | bytes 12292
  4.5 80.3 %copy-start.3 = (bf16[8,64,16]{1,2,0:T(8,128)(2,1)}, bf16[8,64,16]{1,2,0:T(8,128)(2,1)S(1)}, u32[]{:S(2)}) copy-start(bf16[8,64,16]{1,2,0:T(8,128)(2,1)S(1)} %get-tuple-element.11) | copy-start | bytes 49156
  5.2 11.5 %all-to-all-start = ((bf16[8,2,512]{2,1,0:T(2,128)(2,1)}), bf16[8,2,512]{2,1,0:T(2,128)(2,1)S(1)}, u32[]{:S(2)}, u32[]{:S(2)}) async-start(bf16[8,2,512]{2,1,0:T(2,128)(2,1)} %reshape.282), calls=%async_computation | async-start | bytes 32768 | tf_op jit(solution)/shard_map/all_to_all | solution.py:59
  16.7 48.4 %all-to-all-start.1 = ((bf16[8,64,3584]{2,1,0:T(8,128)(2,1)}), bf16[8,64,3584]{2,1,0:T(8,128)(2,1)}, u32[]{:S(2)}, u32[]{:S(2)}) async-start(bf16[8,64,3584]{2,1,0:T(8,128)(2,1)} %convolution_convert_fusion.1), calls=%async_computation.1 | async-start | bytes 7340032 | tf_op jit(solution)/shard_map/all_to_all | solution.py:58
  92.6 6.9 %copy-start.10 = (s32[128]{0:T(128)S(1)}, s32[128]{0:T(128)}, u32[]{:S(2)}) copy-start(s32[128]{0:T(128)} %param.15) | copy-start | bytes 1540
  92.6 141.0 %all-to-all-start.2 = ((bf16[16,80,3584]{2,1,0:T(8,128)(2,1)}), bf16[16,80,3584]{2,1,0:T(8,128)(2,1)}, u32[]{:S(2)}, u32[]{:S(2)}) async-start(bf16[16,80,3584]{2,1,0:T(8,128)(2,1)} %broadcast_select_fusion), calls=%async_computation.2 | async-start | bytes 18350080 | tf_op jit(solution)/shard_map/all_to_all | solution.py:73
  233.7 51.1 %all-to-all-start.5 = ((bf16[128,1,2]{2,1,0:T(2,128)(2,1)}), bf16[128,1,2]{2,1,0:T(2,128)(2,1)S(1)}, u32[]{:S(2)}, u32[]{:S(2)}) async-start(bf16[128,1,2]{2,1,0:T(2,128)(2,1)} %copy.95), calls=%async_computation.5 | async-start | bytes 131072 | tf_op jit(solution)/shard_map/all_to_all | solution.py:116
  284.8 6.9 %copy-start.2 = (bf16[128,576]{0,1:T(8,128)(2,1)S(1)}, bf16[128,576]{0,1:T(8,128)(2,1)}, u32[]{:S(2)}) copy-start(bf16[128,576]{0,1:T(8,128)(2,1)} %param.14) | copy-start | bytes 442372
  284.8 143.3 %all-to-all-start.3 = ((bf16[16,80,3584]{2,1,0:T(8,128)(2,1)}), bf16[16,80,3584]{2,1,0:T(8,128)(2,1)}, u32[]{:S(2)}, u32[]{:S(2)}) async-start(bf16[16,80,3584]{2,1,0:T(8,128)(2,1)} %bitcast.79), calls=%async_computation.3 | async-start | bytes 18350080 | tf_op jit(solution)/shard_map/all_to_all | solution.py:78
  428.0 50.2 %all-to-all-start.6 = ((bf16[128,2,576]{2,1,0:T(2,128)(2,1)}), bf16[128,2,576]{2,1,0:T(2,128)(2,1)S(1)}, u32[]{:S(2)}, u32[]{:S(2)}) async-start(bf16[128,2,576]{2,1,0:T(2,128)(2,1)} %copy.96), calls=%async_computation.6 | async-start | bytes 655360 | tf_op jit(solution)/shard_map/all_to_all | solution.py:115
  478.3 6.1 copy-start.4
  478.3 7.8 %copy-start.5 = (f32[8,64,16]{1,2,0:T(8,128)S(1)}, f32[8,64,16]{1,2,0:T(8,128)}, u32[]{:S(2)}) copy-start(f32[8,64,16]{1,2,0:T(8,128)} %get-tuple-element.10) | copy-start | bytes 98308
  478.3 88.7 %all-to-all-start.4 = ((bf16[8,128,3584]{2,1,0:T(8,128)(2,1)}), bf16[8,128,3584]{2,1,0:T(8,128)(2,1)}, u32[]{:S(2)}, u32[]{:S(2)}) async-start(bf16[8,128,3584]{2,1,0:T(8,128)(2,1)} %bitcast.78), calls=%async_computation.4 | async-start | bytes 14680064 | tf_op jit(solution)/shard_map/all_to_all | solution.py:88
  567.0 43.1 %copy-start.1 = (bf16[128,3584]{1,0:T(8,128)(2,1)S(1)}, bf16[128,3584]{1,0:T(8,128)(2,1)}, u32[]{:S(2)}) copy-start(bf16[128,3584]{1,0:T(8,128)(2,1)} %param.8) | copy-start | bytes 2752516
  583.2 23.2 %copy-start.7 = (s32[8,128]{1,0:T(8,128)S(1)}, s32[8,128]{1,0:T(8,128)}, u32[]{:S(2)}) copy-start(s32[8,128]{1,0:T(8,128)} %copy-done.6) | copy-start | bytes 12292
  583.2 23.2 %copy-start.9 = (pred[128,8]{0,1:T(8,128)(4,1)S(1)}, pred[128,8]{0,1:T(8,128)(4,1)}, u32[]{:S(2)}) copy-start(pred[128,8]{0,1:T(8,128)(4,1)} %copy-done.8) | copy-start | bytes 3076
where the time goes:
time: 612 us; the launch traced here: 610 us
  waiting for transfers between devices  388 us (63%)
  local copies, waits for them, and re-layouts  84.3 us (14%)
  matrix products  51.8 us (8%)
  starting transfers between devices  48.1 us (8%)
  other arithmetic  37.2 us (6%)
    all_to_all x1, waiting for transfers between devices, per_device(): lax.all_to_all(produced, 'local', split_axis=0, concat_axis=0, tiled=True)  135 us
    all_to_all x1, waiting for transfers between devices, per_device(): lax.all_to_all(outgoing, 'local', split_axis=0, concat_axis=0, tiled=True)  133 us
    all_to_all x1, waiting for transfers between devices, per_device(): lax.all_to_all(pair_rows, 'node', split_axis=0, concat_axis=0, tiled=True)  78 us
    all_to_all x1, waiting for transfers between devices, per_device(): lax.all_to_all(send_rows, 'node', split_axis=0, concat_axis=0, tiled=True)  40.3 us
    gather x1, local copies, waits for them, and re-layouts, per_device(): returned[local_pick, slot_pick]  32.2 us
    reduce_sum x1, other arithmetic, per_device(): jnp.sum(pair_gate[:, :, :, None] * home_pairs.astype(jnp.float32), axis=2)  23.2 us
    gather x1, local copies, waits for them, and re-layouts, per_device(): flat_rows[source_row]  19.7 us
    convert_element_type x1, local copies, waits for them, and re-layouts, per_device(): home_pairs.astype(jnp.float32)  16.3 us
  transfers between devices with their start and end apart: 7, of which 5 were waited for; matrix products, arithmetic and copies ran while one was open for 16% of the time, Pallas kernels for 0%

commit v1 on v0

v1 whole, which is shorter than its diff:
```python
import functools

import jax
import jax.numpy as jnp
from jax import lax
from jax.experimental import pallas as pl
from jax.experimental.pallas import tpu as pltpu
from jax.sharding import PartitionSpec as P

MESH = pl.DeviceIdType.MESH
BF16 = jnp.bfloat16
F32 = jnp.float32

NODES = 8
LOCALS = 16
SIDE = 4
CAP = 80
NODE_ROWS = 64
TOK = 128
ROWS = NODES * NODE_ROWS
SLOTS = LOCALS * CAP
WIDTH = 512
TX_SLOTS = 3
LAT_PAD = 640


def iota(shape, dim):
    return lax.broadcasted_iota(jnp.int32, shape, dim)


def mm(a, b):
    return jnp.dot(a, b, preferred_element_type=F32)


def ones_where(mask):
    return jnp.where(mask, 1.0, 0.0)


def wait_for(ref, sem):
    pltpu.make_async_copy(ref, ref, sem).wait()


def rows_at(index, size):
    return pl.ds(pl.multiple_of(index * size, size), size)


def kernel(
    chunks,
    tok,
    ids_t,
    weights_t,
    lat,
    owner,
    wg,
    wu,
    wd,
    moe,
    latent_cache,
    choose,
    choose_t,
    gate_out,
    gate_in,
    pick,
    combine,
    zs,
    zr,
    tx,
    rx,
    ret,
    back,
    acc_gate,
    acc_up,
    hidden,
    wg_buf,
    wu_buf,
    wd_buf,
    lat_s1,
    lat_r1,
    lat_s2,
    lat_r2,
    sem_w,
    sem_z,
    sem_x,
    sem_ret,
    sem_back,
    sem_misc,
):
    node = lax.axis_index("node")
    local = lax.axis_index("local")
    z, core = node // 2, lax.rem(node, 2)
    y, x = local // SIDE, lax.rem(local, SIDE)

    def node_peer(d):
        dz, dc = d // 2, lax.rem(d, 2)
        return lax.rem(z + dz, SIDE) * 2 + lax.rem(core + dc, 2)

    def local_peer(d):
        dy, dx = d // SIDE, lax.rem(d, SIDE)
        return lax.rem(y + dy, SIDE) * SIDE + lax.rem(x + dx, SIDE)

    def to_nodes(src, dst, size, send_sem, recv_sem):
        @pl.loop(1, NODES)
        def _(d):
            peer = node_peer(d)
            pltpu.make_async_remote_copy(
                src_ref=src.at[rows_at(peer, size)],
                dst_ref=dst.at[rows_at(node, size)],
                send_sem=send_sem,
                recv_sem=recv_sem,
                device_id=(peer, local),
                device_id_type=MESH,
            ).start()

    def to_locals(src, dst, size, send_sem, recv_sem):
        @pl.loop(1, LOCALS)
        def _(d):
            peer = local_peer(d)
            pltpu.make_async_remote_copy(
                src_ref=src.at[rows_at(peer, size)],
                dst_ref=dst.at[rows_at(local, size)],
                send_sem=send_sem,
                recv_sem=recv_sem,
                device_id=(node, peer),
                device_id_type=MESH,
            ).start()

    def weights_in(k):
        cols = pl.ds(pl.multiple_of(k * WIDTH, WIDTH), WIDTH)
        slot = lax.rem(k, 2)
        return (
            pltpu.make_async_copy(wg.at[0, cols], wg_buf.at[slot], sem_w.at[0, slot]),
            pltpu.make_async_copy(wu.at[0, cols], wu_buf.at[slot], sem_w.at[1, slot]),
        )

    def down_in(k):
        cols = pl.ds(pl.multiple_of(k * WIDTH, WIDTH), WIDTH)
        slot = lax.rem(k, 2)
        return pltpu.make_async_copy(wd.at[0, :, cols], wd_buf.at[slot], sem_w.at[2, slot])

    barrier = pltpu.get_barrier_semaphore()

    @pl.loop(1, NODES)
    def _(d):
        pl.semaphore_signal(barrier, inc=1, device_id=(node_peer(d), local), device_id_type=MESH)

    @pl.loop(1, LOCALS)
    def _(d):
        pl.semaphore_signal(barrier, inc=1, device_id=(node, local_peer(d)), device_id_type=MESH)

    for copy in weights_in(0) + weights_in(1):
        copy.start()
    down_in(0).start()
    down_in(1).start()

    gates_t = jnp.zeros((TOK, TOK), F32)
    expert_row = iota((TOK, TOK), 0)
    for k in range(ids_t.shape[0]):
        gates_t += jnp.where(ids_t[k : k + 1, :] == expert_row, weights_t[k : k + 1, :], 0.0)
    gates = jnp.transpose(gates_t).astype(BF16)
    hit_t = ones_where(gates_t > 0.0).astype(BF16)
    upto = ones_where(iota((TOK, TOK), 0) <= iota((TOK, TOK), 1)).astype(BF16)
    of_node = ones_where((iota((ROWS, TOK), 0) >> 6) == (iota((ROWS, TOK), 1) >> 4)).astype(BF16)
    reached = ones_where(mm(of_node, hit_t) > 0.0)
    rank = mm(reached.astype(BF16), upto)
    slot_in_node = ((iota((ROWS, TOK), 0) & (NODE_ROWS - 1)) + 1).astype(F32)
    chosen = jnp.where(rank == slot_in_node, reached, 0.0)
    choose[...] = chosen.astype(BF16)
    gate_out[...] = mm(choose[...], gates).astype(BF16)

    pl.semaphore_wait(barrier, NODES - 1 + LOCALS - 1)

    to_nodes(gate_out, gate_in, NODE_ROWS, sem_misc.at[0], sem_misc.at[1])
    gate_in[rows_at(node, NODE_ROWS), :] = gate_out[rows_at(node, NODE_ROWS), :]

    @pl.loop(0, chunks)
    def _(k):
        cols = pl.ds(pl.multiple_of(k * WIDTH, WIDTH), WIDTH)
        zs[k] = mm(choose[...], tok[:, cols]).astype(BF16)
        to_nodes(zs.at[k], zr.at[k], NODE_ROWS, sem_z.at[0, k], sem_z.at[1, k])
        zr[k, rows_at(node, NODE_ROWS), :] = zs[k, rows_at(node, NODE_ROWS), :]

    lat_rows = LOCALS * NODES * 2
    row = iota((lat_rows, TOK), 0)
    owner_of_row = (((row & 15) >> 1) << 4) + (row >> 4)
    owned = ones_where(owner[...] == owner_of_row)
    owned_rank = mm(owned.astype(BF16), upto)
    lat_pick = jnp.where(owned_rank == ((row & 1) + 1).astype(F32), owned, 0.0).astype(BF16)
    lat_s1[...] = mm(lat_pick, lat[...]).astype(BF16)
    to_locals(lat_s1, lat_r1, 16, sem_misc.at[2], sem_misc.at[3])
    lat_r1[rows_at(local, 16), :] = lat_s1[rows_at(local, 16), :]

    choose_t[...] = jnp.transpose(chosen).astype(BF16)

    wait_for(gate_in.at[pl.ds(0, (NODES - 1) * NODE_ROWS)], sem_misc.at[1])
    got = gate_in[...].astype(F32)
    routed = ones_where(got > 0.0)
    before = ones_where(iota((ROWS, ROWS), 1) <= iota((ROWS, ROWS), 0)).astype(BF16)
    count = mm(before, routed.astype(BF16))
    count = jnp.where(routed > 0.0, jnp.minimum(count, 255.0), 0.0).astype(BF16)
    tile = 256

    @pl.loop(0, SLOTS // tile)
    def _(i):
        slot = iota((TOK, tile), 1) + i * tile
        first = (iota((TOK, tile), 0) - node * LOCALS) * CAP
        spread = ones_where((slot >= first) & (slot < first + CAP)).astype(BF16)
        gate_at = mm(gate_in[...], spread)
        count_at = mm(count, spread)
        slot_in_expert = lax.rem(iota((8, tile), 1) + i * tile, CAP)[0:1, :] + 1
        weight = jnp.where(count_at == slot_in_expert.astype(F32), gate_at, 0.0)
        combine[i] = weight.astype(BF16)
        pick[rows_at(i, tile), :] = jnp.transpose(ones_where(weight > 0.0)).astype(BF16)

    def expert_in(k):
        wait_for(rx.at[k, pl.ds(0, SLOTS - CAP)], sem_x.at[1, k])
        for copy in weights_in(k):
            copy.wait()
        slot = lax.rem(k, 2)

        @pl.loop(0, SLOTS // tile)
        def _(i):
            rows = rows_at(i, tile)
            part = rx[k, rows, :]

            @pl.when(k == 0)
            def _():
                acc_gate[rows, :] = mm(part, wg_buf[slot])
                acc_up[rows, :] = mm(part, wu_buf[slot])

            @pl.when(k > 0)
            def _():
                acc_gate[rows, :] += mm(part, wg_buf[slot])
                acc_up[rows, :] += mm(part, wu_buf[slot])

        @pl.when(k + 2 < chunks)
        def _():
            for copy in weights_in(k + 2):
                copy.start()

    @pl.loop(0, chunks + 1)
    def _(k):
        @pl.when(k < chunks)
        def _():
            slot = lax.rem(k, TX_SLOTS)
            wait_for(zr.at[k, pl.ds(0, (NODES - 1) * NODE_ROWS)], sem_z.at[1, k])

            @pl.when(k >= TX_SLOTS)
            def _():
                wait_for(tx.at[slot, pl.ds(0, SLOTS - CAP)], sem_x.at[0, k - TX_SLOTS])

            @pl.loop(0, SLOTS // tile)
            def _(i):
                rows = rows_at(i, tile)
                tx[slot, rows, :] = mm(pick[rows, :], zr[k]).astype(BF16)

            to_locals(tx.at[slot], rx.at[k], CAP, sem_x.at[0, k], sem_x.at[1, k])
            rx[k, rows_at(local, CAP), :] = tx[slot, rows_at(local, CAP), :]

        @pl.when(k >= 1)
        def _():
            expert_in(k - 1)

    wait_for(lat_r1.at[pl.ds(0, lat_rows - 16)], sem_misc.at[3])
    row = iota((lat_rows, lat_rows), 0)
    source = (((row & 31) >> 1) << 4) + ((row >> 5) << 1) + (row & 1)
    turn = ones_where(iota((lat_rows, lat_rows), 1) == source).astype(BF16)
    lat_s2[...] = mm(turn, lat_r1[...]).astype(BF16)
    to_nodes(lat_s2, lat_r2, 32, sem_misc.at[4], sem_misc.at[5])
    lat_r2[rows_at(node, 32), :] = lat_s2[rows_at(node, 32), :]

    @pl.loop(0, SLOTS // tile)
    def _(i):
        rows = rows_at(i, tile)
        gate_act = acc_gate[rows, :]
        hidden[rows, :] = (gate_act / (1.0 + jnp.exp(-gate_act)) * acc_up[rows, :]).astype(BF16)

    @pl.loop(0, chunks)
    def _(k):
        wait_for(zs.at[k, pl.ds(0, (NODES - 1) * NODE_ROWS)], sem_z.at[0, k])

    @pl.loop(chunks - TX_SLOTS, chunks)
    def _(k):
        wait_for(tx.at[0, pl.ds(0, SLOTS - CAP)], sem_x.at[0, k])

    def node_part(k):
        wait_for(ret.at[k, pl.ds(0, SLOTS - CAP)], sem_ret.at[1, k])
        total = mm(combine[0], ret[k, 0:tile, :])
        for i in range(1, SLOTS // tile):
            total += mm(combine[i], ret[k, i * tile : (i + 1) * tile, :])
        zs[k] = total.astype(BF16)
        to_nodes(zs.at[k], back.at[k], NODE_ROWS, sem_back.at[0, k], sem_back.at[1, k])
        back[k, rows_at(node, NODE_ROWS), :] = zs[k, rows_at(node, NODE_ROWS), :]

    def finish(k):
        wait_for(back.at[k, pl.ds(0, (NODES - 1) * NODE_ROWS)], sem_back.at[1, k])
        cols = pl.ds(pl.multiple_of(k * WIDTH, WIDTH), WIDTH)
        moe[:, cols] = mm(choose_t[...], back[k]).astype(BF16)

    @pl.loop(0, chunks + 2)
    def _(k):
        @pl.when(k < chunks)
        def _():
            slot = lax.rem(k, 2)
            down_in(k).wait()

            @pl.loop(0, SLOTS // tile)
            def _(i):
                rows = rows_at(i, tile)
                rx[k, rows, :] = mm(hidden[rows, :], wd_buf[slot]).astype(BF16)

            to_locals(rx.at[k], ret.at[k], CAP, sem_ret.at[0, k], sem_ret.at[1, k])
            ret[k, rows_at(local, CAP), :] = rx[k, rows_at(local, CAP), :]

            @pl.when(k + 2 < chunks)
            def _():
                down_in(k + 2).start()

        @pl.when((k >= 1) & (k < chunks + 1))
        def _():
            node_part(k - 1)

        @pl.when(k >= 2)
        def _():
            finish(k - 2)

    wait_for(lat_r2.at[pl.ds(0, lat_rows - 32)], sem_misc.at[5])
    arrived = lat_r2[...]
    mark = ones_where(iota((8, LAT_PAD), 1) == latent_cache.shape[1]).astype(BF16)
    live = lax.dot_general(mark, arrived, (((1,), (1,)), ((), ())), preferred_element_type=F32)
    upto_lat = ones_where(iota((lat_rows, lat_rows), 0) <= iota((lat_rows, lat_rows), 1))
    place = mm(live.astype(BF16), upto_lat.astype(BF16))
    wanted = (iota((TOK, lat_rows), 0) + 1).astype(F32)
    settle = jnp.where(place[0:1, :] == wanted, live[0:1, :], 0.0).astype(BF16)
    settled = mm(settle, arrived).astype(BF16)
    latent_cache[...] = settled[:, : latent_cache.shape[1]]

    @pl.loop(0, chunks)
    def _(k):
        wait_for(rx.at[k, pl.ds(0, SLOTS - CAP)], sem_ret.at[0, k])
        wait_for(zs.at[k, pl.ds(0, (NODES - 1) * NODE_ROWS)], sem_back.at[0, k])

    wait_for(gate_out.at[pl.ds(0, (NODES - 1) * NODE_ROWS)], sem_misc.at[0])
    wait_for(lat_s1.at[pl.ds(0, lat_rows - 16)], sem_misc.at[2])
    wait_for(lat_s2.at[pl.ds(0, lat_rows - 32)], sem_misc.at[4])


def per_device(tokens, ids, weights, wg, wu, wd, latent_rows, latent_owner):
    count, width = tokens.shape
    lat_width = latent_rows.shape[1]
    hidden_width = wg.shape[2]
    chunks = width // WIDTH
    lat = jnp.concatenate(
        [
            latent_rows,
            jnp.ones((count, 1), BF16),
            jnp.zeros((count, LAT_PAD - lat_width - 1), BF16),
        ],
        axis=1,
    )
    vmem = pl.BlockSpec(memory_space=pltpu.VMEM)
    hbm = pl.BlockSpec(memory_space=pl.ANY)
    lat_all = LOCALS * NODES * 2
    dma = pltpu.SemaphoreType.DMA
    return pl.pallas_call(
        functools.partial(kernel, chunks),
        out_shape=(
            jax.ShapeDtypeStruct((count, width), BF16),
            jax.ShapeDtypeStruct((count, lat_width), BF16),
        ),
        in_specs=[vmem] * 5 + [hbm] * 3,
        out_specs=(vmem, vmem),
        scratch_shapes=[
            pltpu.VMEM((ROWS, TOK), BF16),
            pltpu.VMEM((TOK, ROWS), BF16),
            pltpu.VMEM((ROWS, TOK), BF16),
            pltpu.VMEM((ROWS, TOK), BF16),
            pltpu.VMEM((SLOTS, ROWS), BF16),
            pltpu.VMEM((SLOTS // 256, ROWS, 256), BF16),
            pltpu.VMEM((chunks, ROWS, WIDTH), BF16),
            pltpu.VMEM((chunks, ROWS, WIDTH), BF16),
            pltpu.VMEM((TX_SLOTS, SLOTS, WIDTH), BF16),
            pltpu.VMEM((chunks, SLOTS, WIDTH), BF16),
            pltpu.VMEM((chunks, SLOTS, WIDTH), BF16),
            pltpu.VMEM((chunks, ROWS, WIDTH), BF16),
            pltpu.VMEM((SLOTS, hidden_width), F32),
            pltpu.VMEM((SLOTS, hidden_width), F32),
            pltpu.VMEM((SLOTS, hidden_width), BF16),
            pltpu.VMEM((2, WIDTH, hidden_width), BF16),
            pltpu.VMEM((2, WIDTH, hidden_width), BF16),
            pltpu.VMEM((2, hidden_width, WIDTH), BF16),
            pltpu.VMEM((lat_all, LAT_PAD), BF16),
            pltpu.VMEM((lat_all, LAT_PAD), BF16),
            pltpu.VMEM((lat_all, LAT_PAD), BF16),
            pltpu.VMEM((lat_all, LAT_PAD), BF16),
            dma((3, 2)),
            dma((2, chunks)),
            dma((2, chunks)),
            dma((2, chunks)),
            dma((2, chunks)),
            dma((6,)),
        ],
        compiler_params=pltpu.CompilerParams(
            collective_id=0, has_side_effects=True, vmem_limit_bytes=62 * 2**20
        ),
        cost_estimate=pl.CostEstimate(
            flops=6 * SLOTS * width * hidden_width,
            bytes_accessed=6 * width * hidden_width,
            transcendentals=SLOTS * hidden_width,
        ),
        name="moe_exchange",
    )(
        tokens,
        jnp.transpose(ids),
        jnp.transpose(weights).astype(F32),
        lat,
        latent_owner.reshape(1, count),
        wg,
        wu,
        wd,
    )


def solution(mesh):
    rows = P(("node", "local"), None)
    experts = P(("node", "local"), None, None)
    return jax.shard_map(
        per_device,
        mesh=mesh,
        in_specs=(rows, rows, rows, experts, experts, experts, rows, P(("node", "local"))),
        out_specs=(rows, rows),
        check_vma=False,
    )
```

time: 612 us -> 277 us (0.45)
  waiting for transfers between devices: 388 us -> 0 us
  Pallas kernels: 0 us -> 269 us
  local copies, waits for them, and re-layouts: 84.3 us -> 5.07 us
  matrix products: 51.8 us -> 0 us
  starting transfers between devices: 48.1 us -> 0 us
  other arithmetic: 37.2 us -> 1.99 us
    all_to_all x7 -> x0, waiting for transfers between devices: 388 us -> none  [the longest x1 135 us: per_device(): lax.all_to_all(produced, 'local', split_axis=0, concat_axis=0, tiled=True)]
    pallas_call x0 -> x1, Pallas kernels: none -> 269 us  [per_device(): pl.pallas_call(functools.partial(kernel, chunks), out_shape=(jax.ShapeDty...]
    gather x7 -> x0, local copies, waits for them, and re-layouts: 61.1 us -> none  [the longest x1 32.2 us: per_device(): returned[local_pick, slot_pick]]
    dot_general x8 -> x0, matrix products: 51.8 us -> none  [the longest x1 14.9 us: expert_block(): jnp.dot(flat_in, gate_weight[0], preferred_element_type=jnp.float32)]
    all_to_all x7 -> x0, starting transfers between devices: 48.1 us -> none  [the longest x1 8.37 us: per_device(): lax.all_to_all(lat_send, ('node', 'local'), split_axis=0, concat_axis=0,...]
    reduce_sum x5 -> x0, other arithmetic: 24.3 us -> none  [the longest x1 23.2 us: per_device(): jnp.sum(pair_gate[:, :, :, None] * home_pairs.astype(jnp.float32), axis=2)]
    convert_element_type x7 -> x0, local copies, waits for them, and re-layouts: 19.5 us -> none  [the longest x1 16.3 us: per_device(): home_pairs.astype(jnp.float32)]
    select_n x2 -> x0, other arithmetic: 7.86 us -> none  [the longest x1 7.86 us: per_device(): jnp.where(filled[:, :, None], flat_rows[source_row], jnp.zeros((), jnp.bf...]
  transfers between devices with their start and end apart: 7 -> 0, of which waited for: 5 -> 0; matrix products, arithmetic and copies ran while one was open for 16% -> 0% of each run, Pallas kernels for 0% -> 0%
where the time goes in v1:
time: 277 us; the launch traced here: 276 us
  Pallas kernels  269 us (97%)
  local copies, waits for them, and re-layouts  5.07 us (2%)
    pallas_call x1, Pallas kernels, per_device(): pl.pallas_call(functools.partial(kernel, chunks), out_shape=(jax.ShapeDty...  269 us

profile of v1, /device:TPU:1, one launch (start us, length us, event | category | flops | bytes accessed | tf_op | source)
XLA Modules:
  0.0 276.5 jit_solution(13606011391624825437)
XLA Ops:
  0.6 0.1 pad.2.clone
  0.7 0.1 pad.1.clone
  0.8 1.3 convert_bitcast_fusion.weights_t
  2.1 1.1 copy.10
  3.1 0.7 maximum_maximum_fusion.lat
  3.8 268.8 %moe_exchange.1 = (bf16[128,3584]{1,0:T(8,128)(2,1)}, bf16[128,576]{1,0:T(8,128)(2,1)}) custom-call(bf16[128,3584]{1,0:T(8,128)(2,1)} %tok.1, s32[8,128]{1,0:T(8,128)} %bitcast.5, f32[8,128]{1,0:T(8,128)} %convert_bitcast_fusion.weights_t, bf16[128,640]{1,0:T(8,128)(2,1)} %maximum_maximum_fusion.lat, s32[1,128]{1,0:T(1,128)} %bitcast.6, ...), custom_call_target="tpu_custom_call" | custom-call | flops 28185722880 | bytes 22020096 | tf_op jit(solution)/shard_map/moe_exchange/pallas_call | solution.py:364
  272.6 1.7 copy.11
  274.3 2.2 copy.13
  (1 shorter events, 0.0 us)

commit v2 on v1

--- a/solution.py
+++ b/solution.py
@@ -19,8 +19,14 @@
 TOK = 128
 ROWS = NODES * NODE_ROWS
 SLOTS = LOCALS * CAP
-WIDTH = 512
-TX_SLOTS = 3
+GROUP = SIDE * CAP
+WIDTH = 256
+TX_SLOTS = 4
+AHEAD = 4
+EXPERT_LAG = 2
+PART_LAG = 3
+HOME_LAG = 5
+STRIDE = 3
 LAT_PAD = 640
 
 
@@ -30,6 +36,10 @@
 
 def mm(a, b):
     return jnp.dot(a, b, preferred_element_type=F32)
+
+
+def mm_nt(a, b):
+    return lax.dot_general(a, b, (((1,), (1,)), ((), ())), preferred_element_type=F32)
 
 
 def ones_where(mask):
@@ -49,7 +59,7 @@
     tok,
     ids_t,
     weights_t,
-    lat,
+    lat_t,
     owner,
     wg,
     wu,
@@ -74,13 +84,15 @@
     wg_buf,
     wu_buf,
     wd_buf,
+    lat_pad,
     lat_s1,
     lat_r1,
     lat_s2,
     lat_r2,
     sem_w,
     sem_z,
-    sem_x,
+    sem_tx,
+    sem_rx,
     sem_ret,
     sem_back,
     sem_misc,
@@ -114,7 +126,7 @@
     def to_locals(src, dst, size, send_sem, recv_sem):
         @pl.loop(1, LOCALS)
         def _(d):
-            peer = local_peer(d)
+            peer = local_peer(lax.rem(d * STRIDE, LOCALS))
             pltpu.make_async_remote_copy(
                 src_ref=src.at[rows_at(peer, size)],
                 dst_ref=dst.at[rows_at(local, size)],
@@ -124,6 +136,29 @@
                 device_id_type=MESH,
             ).start()
 
+    def send_rows(k, slot):
+        @pl.loop(1, LOCALS)
+        def _(d):
+            turn = lax.rem(d * STRIDE, LOCALS)
+            peer = local_peer(turn)
+            pltpu.make_async_remote_copy(
+                src_ref=tx.at[slot, rows_at(peer, CAP)],
+                dst_ref=rx.at[k, rows_at(local, CAP)],
+                send_sem=sem_tx.at[k],
+                recv_sem=sem_rx.at[k, lax.rem(SIDE - turn // SIDE, SIDE)],
+                device_id=(node, peer),
+                device_id_type=MESH,
+            ).start()
+
+    def wait_group(k, g):
+        @pl.when(g == 0)
+        def _():
+            wait_for(rx.at[k, pl.ds(0, GROUP - CAP)], sem_rx.at[k, g])
+
+        @pl.when(g > 0)
+        def _():
+            wait_for(rx.at[k, pl.ds(0, GROUP)], sem_rx.at[k, g])
+
     def weights_in(k):
         cols = pl.ds(pl.multiple_of(k * WIDTH, WIDTH), WIDTH)
         slot = lax.rem(k, 2)
@@ -152,10 +187,11 @@
     down_in(0).start()
     down_in(1).start()
 
+    given = weights_t[...].astype(F32)
     gates_t = jnp.zeros((TOK, TOK), F32)
     expert_row = iota((TOK, TOK), 0)
     for k in range(ids_t.shape[0]):
-        gates_t += jnp.where(ids_t[k : k + 1, :] == expert_row, weights_t[k : k + 1, :], 0.0)
+        gates_t += jnp.where(ids_t[k : k + 1, :] == expert_row, given[k : k + 1, :], 0.0)
     gates = jnp.transpose(gates_t).astype(BF16)
     hit_t = ones_where(gates_t > 0.0).astype(BF16)
     upto = ones_where(iota((TOK, TOK), 0) <= iota((TOK, TOK), 1)).astype(BF16)
@@ -172,22 +208,15 @@
     to_nodes(gate_out, gate_in, NODE_ROWS, sem_misc.at[0], sem_misc.at[1])
     gate_in[rows_at(node, NODE_ROWS), :] = gate_out[rows_at(node, NODE_ROWS), :]
 
-    @pl.loop(0, chunks)
-    def _(k):
+    def node_send(k):
         cols = pl.ds(pl.multiple_of(k * WIDTH, WIDTH), WIDTH)
         zs[k] = mm(choose[...], tok[:, cols]).astype(BF16)
         to_nodes(zs.at[k], zr.at[k], NODE_ROWS, sem_z.at[0, k], sem_z.at[1, k])
         zr[k, rows_at(node, NODE_ROWS), :] = zs[k, rows_at(node, NODE_ROWS), :]
 
-    lat_rows = LOCALS * NODES * 2
-    row = iota((lat_rows, TOK), 0)
-    owner_of_row = (((row & 15) >> 1) << 4) + (row >> 4)
-    owned = ones_where(owner[...] == owner_of_row)
-    owned_rank = mm(owned.astype(BF16), upto)
-    lat_pick = jnp.where(owned_rank == ((row & 1) + 1).astype(F32), owned, 0.0).astype(BF16)
-    lat_s1[...] = mm(lat_pick, lat[...]).astype(BF16)
-    to_locals(lat_s1, lat_r1, 16, sem_misc.at[2], sem_misc.at[3])
-    lat_r1[rows_at(local, 16), :] = lat_s1[rows_at(local, 16), :]
+    @pl.loop(0, AHEAD)
+    def _(k):
+        node_send(k)
 
     choose_t[...] = jnp.transpose(chosen).astype(BF16)
 
@@ -211,15 +240,52 @@
         combine[i] = weight.astype(BF16)
         pick[rows_at(i, tile), :] = jnp.transpose(ones_where(weight > 0.0)).astype(BF16)
 
+    lat_rows = LOCALS * NODES * 2
+
+    def latent_first():
+        width = latent_cache.shape[0]
+        lat_pad[0:width, :] = lat_t[...]
+        lat_pad[width:, :] = ones_where(iota((LAT_PAD - width, TOK), 0) == 0).astype(BF16)
+        row = iota((lat_rows, TOK), 0)
+        owner_of_row = (((row & 15) >> 1) << 4) + (row >> 4)
+        owned = ones_where(owner[...] == owner_of_row)
+        upto = ones_where(iota((TOK, TOK), 0) <= iota((TOK, TOK), 1)).astype(BF16)
+        rank = mm(owned.astype(BF16), upto)
+        lat_pick = jnp.where(rank == ((row & 1) + 1).astype(F32), owned, 0.0).astype(BF16)
+        lat_s1[...] = mm_nt(lat_pick, lat_pad[...]).astype(BF16)
+        to_locals(lat_s1, lat_r1, 16, sem_misc.at[2], sem_misc.at[3])
+        lat_r1[rows_at(local, 16), :] = lat_s1[rows_at(local, 16), :]
+
+    def latent_second():
+        wait_for(lat_r1.at[pl.ds(0, lat_rows - 16)], sem_misc.at[3])
+        row = iota((lat_rows, lat_rows), 0)
+        source = (((row & 31) >> 1) << 4) + ((row >> 5) << 1) + (row & 1)
+        turn = ones_where(iota((lat_rows, lat_rows), 1) == source).astype(BF16)
+        lat_s2[...] = mm(turn, lat_r1[...]).astype(BF16)
+        to_nodes(lat_s2, lat_r2, 32, sem_misc.at[4], sem_misc.at[5])
+        lat_r2[rows_at(node, 32), :] = lat_s2[rows_at(node, 32), :]
+
+    def latent_third():
+        wait_for(lat_r2.at[pl.ds(0, lat_rows - 32)], sem_misc.at[5])
+        arrived = lat_r2[...]
+        mark = ones_where(iota((8, LAT_PAD), 1) == latent_cache.shape[0]).astype(BF16)
+        live = mm_nt(mark, arrived)
+        upto = ones_where(iota((lat_rows, lat_rows), 0) <= iota((lat_rows, lat_rows), 1))
+        place = mm(live.astype(BF16), upto.astype(BF16))
+        wanted = (iota((TOK, lat_rows), 0) + 1).astype(F32)
+        settle = jnp.where(place[0:1, :] == wanted, live[0:1, :], 0.0).astype(BF16)
+        settled = jnp.transpose(mm(settle, arrived))
+        latent_cache[...] = settled[0 : latent_cache.shape[0], :].astype(BF16)
+
     def expert_in(k):
-        wait_for(rx.at[k, pl.ds(0, SLOTS - CAP)], sem_x.at[1, k])
         for copy in weights_in(k):
             copy.wait()
         slot = lax.rem(k, 2)
 
-        @pl.loop(0, SLOTS // tile)
-        def _(i):
-            rows = rows_at(i, tile)
+        @pl.loop(0, SIDE)
+        def _(g):
+            wait_group(k, g)
+            rows = rows_at(lax.rem(y + g, SIDE), GROUP)
             part = rx[k, rows, :]
 
             @pl.when(k == 0)
@@ -237,42 +303,77 @@
             for copy in weights_in(k + 2):
                 copy.start()
 
-    @pl.loop(0, chunks + 1)
+    def expert_rows(k):
+        slot = lax.rem(k, TX_SLOTS)
+        wait_for(zr.at[k, pl.ds(0, (NODES - 1) * NODE_ROWS)], sem_z.at[1, k])
+
+        @pl.when(k >= TX_SLOTS)
+        def _():
+            wait_for(tx.at[slot, pl.ds(0, SLOTS - CAP)], sem_tx.at[k - TX_SLOTS])
+
+        @pl.loop(0, SLOTS // tile)
+        def _(i):
+            rows = rows_at(i, tile)
+            tx[slot, rows, :] = mm(pick[rows, :], zr[k]).astype(BF16)
+
+        send_rows(k, slot)
+        rx[k, rows_at(local, CAP), :] = tx[slot, rows_at(local, CAP), :]
+
+    @pl.loop(0, chunks - 1 + EXPERT_LAG)
     def _(k):
         @pl.when(k < chunks)
         def _():
-            slot = lax.rem(k, TX_SLOTS)
-            wait_for(zr.at[k, pl.ds(0, (NODES - 1) * NODE_ROWS)], sem_z.at[1, k])
-
-            @pl.when(k >= TX_SLOTS)
+            expert_rows(k)
+
+        @pl.when(k + AHEAD < chunks)
+        def _():
+            node_send(k + AHEAD)
+
+        @pl.when(k == 1)
+        def _():
+            latent_first()
+
+        @pl.when(k == 6)
+        def _():
+            latent_second()
+
+        @pl.when(k >= EXPERT_LAG)
+        def _():
+            expert_in(k - EXPERT_LAG)
+
+    last = chunks - 1
+    for copy in weights_in(last):
+        copy.wait()
+    down_in(0).wait()
+
+    @pl.loop(0, SIDE)
+    def _(g):
+        wait_group(last, g)
+        there = lax.rem(y + g, SIDE)
+        rows = rows_at(there, GROUP)
+        part = rx[last, rows, :]
+        gate_act = acc_gate[rows, :] + mm(part, wg_buf[last % 2])
+        up_act = acc_up[rows, :] + mm(part, wu_buf[last % 2])
+        hidden[rows, :] = (gate_act / (1.0 + jnp.exp(-gate_act)) * up_act).astype(BF16)
+        rx[0, rows, :] = mm(hidden[rows, :], wd_buf[0]).astype(BF16)
+
+        @pl.loop(0, SIDE)
+        def _(dx):
+            peer = there * SIDE + lax.rem(x + dx, SIDE)
+
+            @pl.when(g + dx > 0)
             def _():
-                wait_for(tx.at[slot, pl.ds(0, SLOTS - CAP)], sem_x.at[0, k - TX_SLOTS])
-
-            @pl.loop(0, SLOTS // tile)
-            def _(i):
-                rows = rows_at(i, tile)
-                tx[slot, rows, :] = mm(pick[rows, :], zr[k]).astype(BF16)
-
-            to_locals(tx.at[slot], rx.at[k], CAP, sem_x.at[0, k], sem_x.at[1, k])
-            rx[k, rows_at(local, CAP), :] = tx[slot, rows_at(local, CAP), :]
-
-        @pl.when(k >= 1)
-        def _():
-            expert_in(k - 1)
-
-    wait_for(lat_r1.at[pl.ds(0, lat_rows - 16)], sem_misc.at[3])
-    row = iota((lat_rows, lat_rows), 0)
-    source = (((row & 31) >> 1) << 4) + ((row >> 5) << 1) + (row & 1)
-    turn = ones_where(iota((lat_rows, lat_rows), 1) == source).astype(BF16)
-    lat_s2[...] = mm(turn, lat_r1[...]).astype(BF16)
-    to_nodes(lat_s2, lat_r2, 32, sem_misc.at[4], sem_misc.at[5])
-    lat_r2[rows_at(node, 32), :] = lat_s2[rows_at(node, 32), :]
-
-    @pl.loop(0, SLOTS // tile)
-    def _(i):
-        rows = rows_at(i, tile)
-        gate_act = acc_gate[rows, :]
-        hidden[rows, :] = (gate_act / (1.0 + jnp.exp(-gate_act)) * acc_up[rows, :]).astype(BF16)
+                pltpu.make_async_remote_copy(
+                    src_ref=rx.at[0, rows_at(peer, CAP)],
+                    dst_ref=ret.at[0, rows_at(local, CAP)],
+                    send_sem=sem_ret.at[0, 0],
+                    recv_sem=sem_ret.at[1, 0],
+                    device_id=(node, peer),
+                    device_id_type=MESH,
+                ).start()
+
+    ret[0, rows_at(local, CAP), :] = rx[0, rows_at(local, CAP), :]
+    down_in(2).start()
 
     @pl.loop(0, chunks)
     def _(k):
@@ -280,7 +381,7 @@
 
     @pl.loop(chunks - TX_SLOTS, chunks)
     def _(k):
-        wait_for(tx.at[0, pl.ds(0, SLOTS - CAP)], sem_x.at[0, k])
+        wait_for(tx.at[0, pl.ds(0, SLOTS - CAP)], sem_tx.at[k])
 
     def node_part(k):
         wait_for(ret.at[k, pl.ds(0, SLOTS - CAP)], sem_ret.at[1, k])
@@ -296,16 +397,16 @@
         cols = pl.ds(pl.multiple_of(k * WIDTH, WIDTH), WIDTH)
         moe[:, cols] = mm(choose_t[...], back[k]).astype(BF16)
 
-    @pl.loop(0, chunks + 2)
+    @pl.loop(1, chunks + HOME_LAG)
     def _(k):
         @pl.when(k < chunks)
         def _():
             slot = lax.rem(k, 2)
             down_in(k).wait()
 
-            @pl.loop(0, SLOTS // tile)
+            @pl.loop(0, SIDE)
             def _(i):
-                rows = rows_at(i, tile)
+                rows = rows_at(i, GROUP)
                 rx[k, rows, :] = mm(hidden[rows, :], wd_buf[slot]).astype(BF16)
 
             to_locals(rx.at[k], ret.at[k], CAP, sem_ret.at[0, k], sem_ret.at[1, k])
@@ -315,24 +416,17 @@
             def _():
                 down_in(k + 2).start()
 
-        @pl.when((k >= 1) & (k < chunks + 1))
-        def _():
-            node_part(k - 1)
-
-        @pl.when(k >= 2)
-        def _():
-            finish(k - 2)
-
-    wait_for(lat_r2.at[pl.ds(0, lat_rows - 32)], sem_misc.at[5])
-    arrived = lat_r2[...]
-    mark = ones_where(iota((8, LAT_PAD), 1) == latent_cache.shape[1]).astype(BF16)
-    live = lax.dot_general(mark, arrived, (((1,), (1,)), ((), ())), preferred_element_type=F32)
-    upto_lat = ones_where(iota((lat_rows, lat_rows), 0) <= iota((lat_rows, lat_rows), 1))
-    place = mm(live.astype(BF16), upto_lat.astype(BF16))
-    wanted = (iota((TOK, lat_rows), 0) + 1).astype(F32)
-    settle = jnp.where(place[0:1, :] == wanted, live[0:1, :], 0.0).astype(BF16)
-    settled = mm(settle, arrived).astype(BF16)
-    latent_cache[...] = settled[:, : latent_cache.shape[1]]
+        @pl.when((k >= PART_LAG) & (k < chunks + PART_LAG))
+        def _():
+            node_part(k - PART_LAG)
+
+        @pl.when(k == 6)
+        def _():
+            latent_third()
+
+        @pl.when(k >= HOME_LAG)
+        def _():
+            finish(k - HOME_LAG)
 
     @pl.loop(0, chunks)
     def _(k):
@@ -349,23 +443,15 @@
     lat_width = latent_rows.shape[1]
     hidden_width = wg.shape[2]
     chunks = width // WIDTH
-    lat = jnp.concatenate(
-        [
-            latent_rows,
-            jnp.ones((count, 1), BF16),
-            jnp.zeros((count, LAT_PAD - lat_width - 1), BF16),
-        ],
-        axis=1,
-    )
     vmem = pl.BlockSpec(memory_space=pltpu.VMEM)
     hbm = pl.BlockSpec(memory_space=pl.ANY)
     lat_all = LOCALS * NODES * 2
     dma = pltpu.SemaphoreType.DMA
-    return pl.pallas_call(
+    moe, cache_t = pl.pallas_call(
         functools.partial(kernel, chunks),
         out_shape=(
             jax.ShapeDtypeStruct((count, width), BF16),
-            jax.ShapeDtypeStruct((count, lat_width), BF16),
+            jax.ShapeDtypeStruct((lat_width, count), BF16),
         ),
         in_specs=[vmem] * 5 + [hbm] * 3,
         out_specs=(vmem, vmem),
@@ -388,13 +474,15 @@
             pltpu.VMEM((2, WIDTH, hidden_width), BF16),
             pltpu.VMEM((2, WIDTH, hidden_width), BF16),
             pltpu.VMEM((2, hidden_width, WIDTH), BF16),
+            pltpu.VMEM((LAT_PAD, count), BF16),
             pltpu.VMEM((lat_all, LAT_PAD), BF16),
             pltpu.VMEM((lat_all, LAT_PAD), BF16),
             pltpu.VMEM((lat_all, LAT_PAD), BF16),
             pltpu.VMEM((lat_all, LAT_PAD), BF16),
             dma((3, 2)),
             dma((2, chunks)),
-            dma((2, chunks)),
+            dma((chunks,)),
+            dma((chunks, SIDE)),
             dma((2, chunks)),
             dma((2, chunks)),
             dma((6,)),
@@ -411,13 +499,14 @@
     )(
         tokens,
         jnp.transpose(ids),
-        jnp.transpose(weights).astype(F32),
-        lat,
+        jnp.transpose(weights),
+        jnp.transpose(latent_rows),
         latent_owner.reshape(1, count),
         wg,
         wu,
         wd,
     )
+    return moe, jnp.transpose(cache_t)
 
 
 def solution(mesh):

time: 277 us -> 244 us (0.88)
  the two profiles are of different devices: /device:TPU:1 before, /device:TPU:9 now
where the time goes in v2:
time: 244 us
  Pallas kernels  239 us (98%)
  local copies, waits for them, and re-layouts  3.74 us (2%)
    pallas_call x1, Pallas kernels, per_device(): pl.pallas_call(functools.partial(kernel, chunks), out_shape=(jax.ShapeDty...  239 us

profile of v2, /device:TPU:9, one launch (start us, length us, event | category | flops | bytes accessed | tf_op | source)
XLA Modules:
  0.0 243.5 jit_solution(10249314962637431594)
XLA Ops:
  0.6 239.1 %moe_exchange.1 = (bf16[128,3584]{1,0:T(8,128)(2,1)}, bf16[576,128]{1,0:T(8,128)(2,1)}) custom-call(bf16[128,3584]{1,0:T(8,128)(2,1)} %tok.1, s32[8,128]{1,0:T(8,128)} %bitcast.7, bf16[8,128]{1,0:T(8,128)(2,1)} %bitcast.8, bf16[576,128]{1,0:T(8,128)(2,1)} %bitcast.6, s32[1,128]{1,0:T(1,128)} %bitcast.9, bf16[1,3584,1024]{2,1,0:T(8,128)(2,1)} %wg.1, ...), custom_call_target="tpu_custom_call" | custom-call | flops 28185722880 | bytes 22020096 | tf_op jit(solution)/shard_map/moe_exchange/pallas_call | solution.py:450
  239.8 2.2 copy.12
  241.9 1.6 copy.13

commit v3 on v2

v3 whole, which is shorter than its diff:
```python
import functools

import jax
import jax.numpy as jnp
from jax import lax
from jax.experimental import pallas as pl
from jax.experimental.pallas import tpu as pltpu
from jax.sharding import PartitionSpec as P

MESH = pl.DeviceIdType.MESH
BF16 = jnp.bfloat16
F32 = jnp.float32

NODES = 8
LOCALS = 16
SIDE = 4
TYPES = 4
COVER = 8
CAP = 80
NODE_ROWS = 64
PAIR_ROWS = 2 * NODE_ROWS
TOK = 128
ROWS = NODES * NODE_ROWS
SLOTS = LOCALS * CAP
HALF = COVER * CAP
GROUP = SIDE * CAP
REMOTE = 2 * (COVER - 1)
WIDTH = 256
TX_SLOTS = 6
ZS_SLOTS = 4
AHEAD = 3
EXPERT_LAG = 4
PART_LAG = 5
HOME_LAG = 7
END_LAG = 8
STRIDE = 3
BUILD = 128
LAT_PAD = 640


def iota(shape, dim):
    return lax.broadcasted_iota(jnp.int32, shape, dim)


def mm(a, b):
    return jnp.dot(a, b, preferred_element_type=F32)


def mm_nt(a, b):
    return lax.dot_general(a, b, (((1,), (1,)), ((), ())), preferred_element_type=F32)


def ones_where(mask):
    return jnp.where(mask, 1.0, 0.0)


def wait_for(ref, sem):
    pltpu.make_async_copy(ref, ref, sem).wait()


def rows_at(index, size):
    return pl.ds(pl.multiple_of(index * size, size), size)


def kernel(
    chunks,
    tok,
    ids_t,
    weights_t,
    lat_t,
    owner,
    wg,
    wu,
    wd,
    moe,
    latent_cache,
    named,
    named_in,
    choose,
    choose_t,
    gates,
    counts,
    gate_out,
    moves,
    shared,
    shared_back,
    zs,
    passed,
    tx,
    rx,
    back,
    acc_gate,
    acc_up,
    hidden,
    wg_buf,
    wu_buf,
    wd_buf,
    lat_pad,
    lat_s1,
    lat_r1,
    lat_s2,
    lat_r2,
    sem_w,
    sem_named,
    sem_gates,
    sem_shared,
    sem_home,
    sem_z,
    sem_tx,
    sem_rx,
    sem_ret,
    sem_back,
    sem_misc,
):
    node = lax.axis_index("node")
    local = lax.axis_index("local")
    z, core = node // 2, lax.rem(node, 2)
    y, x = local // SIDE, lax.rem(local, SIDE)

    def node_peer(d):
        dz, dc = d // 2, lax.rem(d, 2)
        return lax.rem(z + dz, SIDE) * 2 + lax.rem(core + dc, 2)

    def local_peer(d):
        dy, dx = d // SIDE, lax.rem(d, SIDE)
        return lax.rem(y + dy, SIDE) * SIDE + lax.rem(x + dx, SIDE)

    def paired(v, way):
        return (1 - way) * (v + 1 - 2 * lax.rem(v, 2)) + way * (SIDE - 1 - v)

    def kind(k):
        t = lax.rem(k, TYPES)
        return lax.rem(t, 2), t // 2

    def partner_of(py, px, t):
        along_x, way = kind(t)
        return (
            py + (1 - along_x) * (paired(py, way) - py),
            px + along_x * (paired(px, way) - px),
        )

    def partner_at(t):
        py, px = partner_of(y, x, t)
        return py * SIDE + px

    def cover(t, a, b):
        along_x, way = kind(t)
        cy = (1 - along_x) * (y + a * (paired(y, 1 - way) - y)) + along_x * lax.rem(y + b, SIDE)
        cx = along_x * (x + a * (paired(x, 1 - way) - x)) + (1 - along_x) * lax.rem(x + b, SIDE)
        return cy, cx

    def send(src, dst, send_sem, recv_sem, device):
        pltpu.make_async_remote_copy(
            src_ref=src,
            dst_ref=dst,
            send_sem=send_sem,
            recv_sem=recv_sem,
            device_id=device,
            device_id_type=MESH,
        ).start()

    def to_nodes(src, dst, size, send_sem, recv_sem):
        @pl.loop(1, NODES)
        def _(d):
            peer = node_peer(d)
            send(
                src.at[rows_at(peer, size)],
                dst.at[rows_at(node, size)],
                send_sem,
                recv_sem,
                (peer, local),
            )

    def to_locals(src, dst, size, send_sem, recv_sem):
        @pl.loop(1, LOCALS)
        def _(d):
            peer = local_peer(lax.rem(d * STRIDE, LOCALS))
            send(
                src.at[rows_at(peer, size)],
                dst.at[rows_at(local, size)],
                send_sem,
                recv_sem,
                (node, peer),
            )

    def columns(k):
        return pl.ds(pl.multiple_of(k * WIDTH, WIDTH), WIDTH)

    def weights_in(k):
        slot = lax.rem(k, 2)
        return (
            pltpu.make_async_copy(wg.at[0, columns(k)], wg_buf.at[slot], sem_w.at[0, slot]),
            pltpu.make_async_copy(wu.at[0, columns(k)], wu_buf.at[slot], sem_w.at[1, slot]),
        )

    def down_in(k):
        slot = lax.rem(k, 2)
        return pltpu.make_async_copy(wd.at[0, :, columns(k)], wd_buf.at[slot], sem_w.at[2, slot])

    barrier = pltpu.get_barrier_semaphore()

    @pl.loop(1, LOCALS)
    def _(d):
        pl.semaphore_signal(barrier, inc=1, device_id=(node, local_peer(d)), device_id_type=MESH)

    @pl.loop(1, NODES)
    def _(d):
        pl.semaphore_signal(barrier, inc=1, device_id=(node_peer(d), local), device_id_type=MESH)

    for copy in weights_in(0) + weights_in(1):
        copy.start()
    down_in(0).start()
    down_in(1).start()
    named[0 : ids_t.shape[0], :] = ids_t[...].astype(F32)
    named[ids_t.shape[0] :, :] = weights_t[...].astype(F32)

    def route(who, names):
        gates_t = jnp.zeros((TOK, TOK), F32)
        expert_row = iota((TOK, TOK), 0).astype(F32)
        top = ids_t.shape[0]
        for k in range(top):
            hit = names[k : k + 1, :] == expert_row
            gates_t += jnp.where(hit, names[top + k : top + k + 1, :], 0.0)
        hit_t = ones_where(gates_t > 0.0).astype(BF16)
        upto = ones_where(iota((TOK, TOK), 0) <= iota((TOK, TOK), 1)).astype(BF16)
        of_node = ones_where((iota((ROWS, TOK), 0) >> 6) == (iota((ROWS, TOK), 1) >> 4))
        reached = ones_where(mm(of_node.astype(BF16), hit_t) > 0.0)
        rank = mm(reached.astype(BF16), upto)
        slot_in_node = ((iota((ROWS, TOK), 0) & (NODE_ROWS - 1)) + 1).astype(F32)
        choose[who] = jnp.where(rank == slot_in_node, reached, 0.0).astype(BF16)
        return gates_t

    own_gates = jnp.transpose(route(0, named[...])).astype(BF16)
    gate_out[...] = mm(choose[0], own_gates).astype(BF16)

    pl.semaphore_wait(barrier, NODES - 1 + LOCALS - 1)

    to_nodes(gate_out, gates.at[0], NODE_ROWS, sem_misc.at[0], sem_misc.at[1])

    @pl.loop(0, TYPES)
    def _(t):
        there = (node, partner_at(t))
        send(named, named_in.at[t], sem_named.at[0, t], sem_named.at[1, t], there)

    @pl.loop(0, chunks)
    def _(k):
        there = (node, partner_at(k))
        send(
            tok.at[:, columns(k)], shared.at[k], sem_shared.at[0, k], sem_shared.at[1, k], there
        )

    gates[0, rows_at(node, NODE_ROWS), :] = gate_out[rows_at(node, NODE_ROWS), :]

    def put_pair(slot, side, value):
        for n in range(NODES):
            at = n * PAIR_ROWS + side * NODE_ROWS
            zs[slot, at : at + NODE_ROWS, :] = value[n * NODE_ROWS : (n + 1) * NODE_ROWS, :]

    def get_pair(ref, k, side):
        starts = [n * PAIR_ROWS + side * NODE_ROWS for n in range(NODES)]
        return jnp.concatenate([ref[k, at : at + NODE_ROWS, :] for at in starts], axis=0)

    def node_send(k):
        t = lax.rem(k, TYPES)
        slot = lax.rem(k, ZS_SLOTS)

        @pl.when(k < TYPES)
        def _():
            wait_for(named_in.at[t], sem_named.at[1, t])
            route(1 + t, named_in[t])

        @pl.when(k >= ZS_SLOTS)
        def _():
            wait_for(zs.at[slot, pl.ds(0, (NODES - 1) * PAIR_ROWS)], sem_z.at[0, k - ZS_SLOTS])

        put_pair(slot, 0, mm(choose[0], tok[:, columns(k)]).astype(BF16))
        wait_for(shared.at[k], sem_shared.at[1, k])
        put_pair(slot, 1, mm(choose[1 + t], shared[k]).astype(BF16))
        to_nodes(zs.at[slot], passed.at[k], PAIR_ROWS, sem_z.at[0, k], sem_z.at[1, k])
        passed[k, rows_at(node, PAIR_ROWS), :] = zs[slot, rows_at(node, PAIR_ROWS), :]

    def count_rows(who):
        routed = ones_where(gates[who].astype(F32) > 0.0)
        before = ones_where(iota((ROWS, ROWS), 1) <= iota((ROWS, ROWS), 0)).astype(BF16)
        count = mm(before, routed.astype(BF16))
        counts[who] = jnp.where(routed > 0.0, jnp.minimum(count, 255.0), 0.0).astype(BF16)

    def expert_lane(slot, t):
        along_x, way = kind(t)
        i = lax.div(slot, CAP)
        a, b = i >> 2, i & 3
        on_y = y + a * (paired(y, 1 - way) - y)
        on_x = x + a * (paired(x, 1 - way) - x)
        lane_y = on_y * SIDE + ((x + b) & 3)
        lane_x = ((y + b) & 3) * SIDE + on_x
        return node * LOCALS + (1 - along_x) * lane_y + along_x * lane_x

    def build_pick(t):
        @pl.loop(0, 2 * HALF // BUILD)
        def _(j):
            side = j // (HALF // BUILD)
            i = lax.rem(j, HALF // BUILD)
            who = side * (1 + t)
            slot = iota((BUILD, TOK), 0) + i * BUILD
            spread = ones_where(iota((BUILD, TOK), 1) == expert_lane(slot, t)).astype(BF16)
            count_at = mm_nt(spread, counts[who])
            wanted = (lax.rem(iota((BUILD, ROWS), 0) + i * BUILD, CAP) + 1).astype(F32)
            moves[t, side, rows_at(i, BUILD), :] = ones_where(count_at == wanted).astype(BF16)

    def build_combine(t):
        @pl.loop(0, 2 * HALF // BUILD)
        def _(j):
            side = j // (HALF // BUILD)
            i = lax.rem(j, HALF // BUILD)
            who = side * (1 + t)
            slot = iota((TOK, BUILD), 1) + i * BUILD
            spread = ones_where(iota((TOK, BUILD), 0) == expert_lane(slot, t)).astype(BF16)
            count_at = mm(counts[who], spread)
            gate_at = mm(gates[who], spread)
            wanted = (lax.rem(iota((8, BUILD), 1) + i * BUILD, CAP)[0:1, :] + 1).astype(F32)
            weight = jnp.where(count_at == wanted, gate_at, 0.0).astype(BF16)
            for q in range(ROWS // BUILD):
                moves[t, side, rows_at(i, BUILD), q * BUILD : (q + 1) * BUILD] = weight[
                    q * BUILD : (q + 1) * BUILD, :
                ]

    node_send(0)
    wait_for(gates.at[0, pl.ds(0, (NODES - 1) * NODE_ROWS)], sem_misc.at[1])

    @pl.loop(0, TYPES)
    def _(t):
        there = (node, partner_at(t))
        send(gates.at[0], gates.at[1 + t], sem_gates.at[0, t], sem_gates.at[1, t], there)

    count_rows(0)

    @pl.loop(1, AHEAD)
    def _(k):
        node_send(k)

    lat_rows = LOCALS * NODES * 2

    def latent_first():
        width = latent_cache.shape[0]
        lat_pad[0:width, :] = lat_t[...]
        lat_pad[width:, :] = ones_where(iota((LAT_PAD - width, TOK), 0) == 0).astype(BF16)
        row = iota((lat_rows, TOK), 0)
        owner_of_row = (((row & 15) >> 1) << 4) + (row >> 4)
        owned = ones_where(owner[...] == owner_of_row)
        upto = ones_where(iota((TOK, TOK), 0) <= iota((TOK, TOK), 1)).astype(BF16)
        rank = mm(owned.astype(BF16), upto)
        lat_pick = jnp.where(rank == ((row & 1) + 1).astype(F32), owned, 0.0).astype(BF16)
        lat_s1[...] = mm_nt(lat_pick, lat_pad[...]).astype(BF16)
        to_locals(lat_s1, lat_r1, 16, sem_misc.at[2], sem_misc.at[3])
        lat_r1[rows_at(local, 16), :] = lat_s1[rows_at(local, 16), :]

    def latent_second():
        wait_for(lat_r1.at[pl.ds(0, lat_rows - 16)], sem_misc.at[3])
        row = iota((lat_rows, lat_rows), 0)
        source = (((row & 31) >> 1) << 4) + ((row >> 5) << 1) + (row & 1)
        turn = ones_where(iota((lat_rows, lat_rows), 1) == source).astype(BF16)
        lat_s2[...] = mm(turn, lat_r1[...]).astype(BF16)
        to_nodes(lat_s2, lat_r2, 32, sem_misc.at[4], sem_misc.at[5])
        lat_r2[rows_at(node, 32), :] = lat_s2[rows_at(node, 32), :]

    def latent_third():
        wait_for(lat_r2.at[pl.ds(0, lat_rows - 32)], sem_misc.at[5])
        arrived = lat_r2[...]
        mark = ones_where(iota((8, LAT_PAD), 1) == latent_cache.shape[0]).astype(BF16)
        live = mm_nt(mark, arrived)
        upto = ones_where(iota((lat_rows, lat_rows), 0) <= iota((lat_rows, lat_rows), 1))
        place = mm(live.astype(BF16), upto.astype(BF16))
        wanted = (iota((TOK, lat_rows), 0) + 1).astype(F32)
        settle = jnp.where(place[0:1, :] == wanted, live[0:1, :], 0.0).astype(BF16)
        settled = jnp.transpose(mm(settle, arrived))
        latent_cache[...] = settled[0 : latent_cache.shape[0], :].astype(BF16)

    def wait_group(k, cy):
        py, _ = partner_of(y, x, k)
        missing = (cy == y).astype(jnp.int32) + (cy == py).astype(jnp.int32)
        for skipped in range(3):

            @pl.when(missing == skipped)
            def _():
                wait_for(rx.at[k, pl.ds(0, GROUP - skipped * CAP)], sem_rx.at[k, cy])

    def expert_in(k):
        for copy in weights_in(k):
            copy.wait()
        slot = lax.rem(k, 2)

        @pl.loop(0, SIDE)
        def _(g):
            cy = lax.rem(y + g, SIDE)
            wait_group(k, cy)
            rows = rows_at(cy, GROUP)
            part = rx[k, rows, :]

            @pl.when(k == 0)
            def _():
                acc_gate[rows, :] = mm(part, wg_buf[slot])
                acc_up[rows, :] = mm(part, wu_buf[slot])

            @pl.when(k > 0)
            def _():
                acc_gate[rows, :] += mm(part, wg_buf[slot])
                acc_up[rows, :] += mm(part, wu_buf[slot])

        @pl.when(k + 2 < chunks)
        def _():
            for copy in weights_in(k + 2):
                copy.start()

    def expert_rows(k):
        t = lax.rem(k, TYPES)
        slot = lax.rem(k, TX_SLOTS)

        @pl.when(k < TYPES)
        def _():
            wait_for(gates.at[1 + t], sem_gates.at[1, t])
            count_rows(1 + t)
            build_pick(t)

        wait_for(passed.at[k, pl.ds(0, (NODES - 1) * PAIR_ROWS)], sem_z.at[1, k])

        @pl.when(k >= TX_SLOTS)
        def _():
            wait_for(tx.at[slot, pl.ds(0, REMOTE * CAP)], sem_tx.at[k - TX_SLOTS])

        for side in range(2):
            arrived = get_pair(passed, k, side)
            rows = pl.ds(side * HALF, HALF)
            tx[slot, rows, :] = mm(moves[t, side], arrived).astype(BF16)

        py, px = partner_of(y, x, k)

        @pl.loop(0, REMOTE)
        def _(m):
            side = m // (COVER - 1)
            i = 1 + lax.rem(m * STRIDE, COVER - 1)
            ey, ex = cover(k, i // SIDE, lax.rem(i, SIDE))
            cy = y + side * (py - y)
            cx = x + side * (px - x)
            send(
                tx.at[slot, rows_at(side * COVER + i, CAP)],
                rx.at[k, rows_at(cy * SIDE + cx, CAP)],
                sem_tx.at[k],
                sem_rx.at[k, cy],
                (node, ey * SIDE + ex),
            )

        rx[k, rows_at(local, CAP), :] = tx[slot, 0:CAP, :]
        rx[k, rows_at(py * SIDE + px, CAP), :] = tx[slot, HALF : HALF + CAP, :]

    @pl.loop(0, chunks - 1 + EXPERT_LAG)
    def _(k):
        @pl.when(k < chunks)
        def _():
            expert_rows(k)

        @pl.when(k + AHEAD < chunks)
        def _():
            node_send(k + AHEAD)

        @pl.when(k == 4)
        def _():
            latent_first()

        @pl.when(k == 8)
        def _():
            latent_second()

        @pl.when(k >= EXPERT_LAG)
        def _():
            expert_in(k - EXPERT_LAG)

    def send_back(k, a, b, side):
        fy, fx = cover(k, a, b)
        py, px = partner_of(fy, fx, k)
        cy = fy + side * (py - fy)
        cx = fx + side * (px - fx)
        i = a * SIDE + lax.rem(SIDE - b, SIDE)
        send(
            rx.at[k, rows_at(cy * SIDE + cx, CAP)],
            passed.at[k, rows_at(side * COVER + i, CAP)],
            sem_ret.at[0, k],
            sem_ret.at[1, k],
            (node, fy * SIDE + fx),
        )

    def keep_back(k):
        passed[k, 0:CAP, :] = rx[k, rows_at(local, CAP), :]
        passed[k, HALF : HALF + CAP, :] = rx[k, rows_at(partner_at(k), CAP), :]

    last = chunks - 1
    for copy in weights_in(last):
        copy.wait()
    down_in(0).wait()

    @pl.loop(0, SIDE)
    def _(g):
        a, side = lax.rem(g, 2), g // 2
        fy, fx = cover(0, a, 0)
        py, _ = partner_of(fy, fx, 0)
        there = fy + side * (py - fy)
        wait_group(last, there)
        rows = rows_at(there, GROUP)
        part = rx[last, rows, :]
        gate_act = acc_gate[rows, :] + mm(part, wg_buf[last % 2])
        up_act = acc_up[rows, :] + mm(part, wu_buf[last % 2])
        hidden[rows, :] = (gate_act / (1.0 + jnp.exp(-gate_act)) * up_act).astype(BF16)
        rx[0, rows, :] = mm(hidden[rows, :], wd_buf[0]).astype(BF16)

        @pl.loop(0, SIDE)
        def _(b):
            @pl.when(a + b > 0)
            def _():
                send_back(0, a, b, side)

    keep_back(0)
    down_in(2).start()

    @pl.loop(chunks - ZS_SLOTS, chunks)
    def _(k):
        wait_for(zs.at[0, pl.ds(0, (NODES - 1) * PAIR_ROWS)], sem_z.at[0, k])

    @pl.loop(chunks - TX_SLOTS, chunks)
    def _(k):
        wait_for(tx.at[0, pl.ds(0, REMOTE * CAP)], sem_tx.at[k])

    parts = [pl.ds(i * BUILD, BUILD) for i in range(HALF // BUILD)]

    def node_part(k):
        t = lax.rem(k, TYPES)
        slot = lax.rem(k, ZS_SLOTS)

        @pl.when(k < TYPES)
        def _():
            build_combine(t)

        wait_for(passed.at[k, pl.ds(0, REMOTE * CAP)], sem_ret.at[1, k])

        @pl.when(k >= ZS_SLOTS)
        def _():
            wait_for(zs.at[slot, pl.ds(0, (NODES - 1) * PAIR_ROWS)], sem_back.at[0, k - ZS_SLOTS])

        for side in range(2):
            weight = jnp.concatenate(
                [
                    jnp.concatenate(
                        [moves[t, side, part, pl.ds(q * BUILD, BUILD)] for part in parts], axis=1
                    )
                    for q in range(ROWS // BUILD)
                ],
                axis=0,
            )
            total = mm(weight, passed[k, side * HALF : (side + 1) * HALF, :])
            put_pair(slot, side, total.astype(BF16))

        to_nodes(zs.at[slot], back.at[k], PAIR_ROWS, sem_back.at[0, k], sem_back.at[1, k])
        back[k, rows_at(node, PAIR_ROWS), :] = zs[slot, rows_at(node, PAIR_ROWS), :]

    def to_partner(k):
        t = lax.rem(k, TYPES)

        @pl.when(k < TYPES)
        def _():
            choose_t[1 + t] = jnp.transpose(choose[1 + t].astype(F32)).astype(BF16)

        wait_for(back.at[k, pl.ds(0, (NODES - 1) * PAIR_ROWS)], sem_back.at[1, k])
        shared[k] = mm(choose_t[1 + t], get_pair(back, k, 1)).astype(BF16)
        there = (node, partner_at(k))
        send(shared.at[k], shared_back.at[k], sem_home.at[0, k], sem_home.at[1, k], there)

    def finish(k):
        own = mm(choose_t[0], get_pair(back, k, 0))
        wait_for(shared_back.at[k], sem_home.at[1, k])
        moe[:, columns(k)] = (own + shared_back[k].astype(F32)).astype(BF16)

    choose_t[0] = jnp.transpose(choose[0].astype(F32)).astype(BF16)

    @pl.loop(1, chunks + END_LAG)
    def _(k):
        @pl.when(k < chunks)
        def _():
            slot = lax.rem(k, 2)
            down_in(k).wait()

            @pl.loop(0, SIDE)
            def _(i):
                rows = rows_at(i, GROUP)
                rx[k, rows, :] = mm(hidden[rows, :], wd_buf[slot]).astype(BF16)

            @pl.loop(0, REMOTE)
            def _(m):
                j = 1 + lax.rem(m * STRIDE, COVER - 1)
                send_back(k, j // SIDE, lax.rem(j, SIDE), m // (COVER - 1))

            keep_back(k)

            @pl.when(k + 2 < chunks)
            def _():
                down_in(k + 2).start()

        @pl.when((k >= PART_LAG) & (k < chunks + PART_LAG))
        def _():
            node_part(k - PART_LAG)

        @pl.when(k == 9)
        def _():
            latent_third()

        @pl.when((k >= HOME_LAG) & (k < chunks + HOME_LAG))
        def _():
            to_partner(k - HOME_LAG)

        @pl.when(k >= END_LAG)
        def _():
            finish(k - END_LAG)

    @pl.loop(0, chunks)
    def _(k):
        wait_for(shared.at[k], sem_shared.at[0, k])
        wait_for(shared.at[k], sem_home.at[0, k])
        wait_for(rx.at[k, pl.ds(0, REMOTE * CAP)], sem_ret.at[0, k])

    @pl.loop(chunks - ZS_SLOTS, chunks)
    def _(k):
        wait_for(zs.at[0, pl.ds(0, (NODES - 1) * PAIR_ROWS)], sem_back.at[0, k])

    @pl.loop(0, TYPES)
    def _(t):
        wait_for(named, sem_named.at[0, t])
        wait_for(gates.at[0], sem_gates.at[0, t])

    wait_for(gate_out.at[pl.ds(0, (NODES - 1) * NODE_ROWS)], sem_misc.at[0])
    wait_for(lat_s1.at[pl.ds(0, lat_rows - 16)], sem_misc.at[2])
    wait_for(lat_s2.at[pl.ds(0, lat_rows - 32)], sem_misc.at[4])


def per_device(tokens, ids, weights, wg, wu, wd, latent_rows, latent_owner):
    count, width = tokens.shape
    lat_width = latent_rows.shape[1]
    hidden_width = wg.shape[2]
    chunks = width // WIDTH
    vmem = pl.BlockSpec(memory_space=pltpu.VMEM)
    hbm = pl.BlockSpec(memory_space=pl.ANY)
    lat_all = LOCALS * NODES * 2
    dma = pltpu.SemaphoreType.DMA
    moe, cache_t = pl.pallas_call(
        functools.partial(kernel, chunks),
        out_shape=(
            jax.ShapeDtypeStruct((count, width), BF16),
            jax.ShapeDtypeStruct((lat_width, count), BF16),
        ),
        in_specs=[vmem] * 5 + [hbm] * 3,
        out_specs=(vmem, vmem),
        scratch_shapes=[
            pltpu.VMEM((2 * ids.shape[1], TOK), F32),
            pltpu.VMEM((TYPES, 2 * ids.shape[1], TOK), F32),
            pltpu.VMEM((1 + TYPES, ROWS, TOK), BF16),
            pltpu.VMEM((1 + TYPES, TOK, ROWS), BF16),
            pltpu.VMEM((1 + TYPES, ROWS, TOK), BF16),
            pltpu.VMEM((1 + TYPES, ROWS, TOK), BF16),
            pltpu.VMEM((ROWS, TOK), BF16),
            pltpu.VMEM((TYPES, 2, HALF, ROWS), BF16),
            pltpu.VMEM((chunks, TOK, WIDTH), BF16),
            pltpu.VMEM((chunks, TOK, WIDTH), BF16),
            pltpu.VMEM((ZS_SLOTS, NODES * PAIR_ROWS, WIDTH), BF16),
            pltpu.VMEM((chunks, SLOTS, WIDTH), BF16),
            pltpu.VMEM((TX_SLOTS, SLOTS, WIDTH), BF16),
            pltpu.VMEM((chunks, SLOTS, WIDTH), BF16),
            pltpu.VMEM((chunks, NODES * PAIR_ROWS, WIDTH), BF16),
            pltpu.VMEM((SLOTS, hidden_width), F32),
            pltpu.VMEM((SLOTS, hidden_width), F32),
            pltpu.VMEM((SLOTS, hidden_width), BF16),
            pltpu.VMEM((2, WIDTH, hidden_width), BF16),
            pltpu.VMEM((2, WIDTH, hidden_width), BF16),
            pltpu.VMEM((2, hidden_width, WIDTH), BF16),
            pltpu.VMEM((LAT_PAD, count), BF16),
            pltpu.VMEM((lat_all, LAT_PAD), BF16),
            pltpu.VMEM((lat_all, LAT_PAD), BF16),
            pltpu.VMEM((lat_all, LAT_PAD), BF16),
            pltpu.VMEM((lat_all, LAT_PAD), BF16),
            dma((3, 2)),
            dma((2, TYPES)),
            dma((2, TYPES)),
            dma((2, chunks)),
            dma((2, chunks)),
            dma((2, chunks)),
            dma((chunks,)),
            dma((chunks, SIDE)),
            dma((2, chunks)),
            dma((2, chunks)),
            dma((6,)),
        ],
        compiler_params=pltpu.CompilerParams(
            collective_id=0, has_side_effects=True, vmem_limit_bytes=62 * 2**20
        ),
        cost_estimate=pl.CostEstimate(
            flops=6 * SLOTS * width * hidden_width,
            bytes_accessed=6 * width * hidden_width,
            transcendentals=SLOTS * hidden_width,
        ),
        name="moe_exchange",
    )(
        tokens,
        jnp.transpose(ids),
        jnp.transpose(weights),
        jnp.transpose(latent_rows),
        latent_owner.reshape(1, count),
        wg,
        wu,
        wd,
    )
    return moe, jnp.transpose(cache_t)


def solution(mesh):
    rows = P(("node", "local"), None)
    experts = P(("node", "local"), None, None)
    return jax.shard_map(
        per_device,
        mesh=mesh,
        in_specs=(rows, rows, rows, experts, experts, experts, rows, P(("node", "local"))),
        out_specs=(rows, rows),
        check_vma=False,
    )
```

time: 244 us -> 240 us (0.984)
  the two profiles are of different devices: /device:TPU:9 before, /device:TPU:1 now
where the time goes in v3:
time: 240 us
  Pallas kernels  235 us (98%)
  local copies, waits for them, and re-layouts  3.74 us (2%)
    pallas_call x1, Pallas kernels, per_device(): pl.pallas_call(functools.partial(kernel, chunks), out_shape=(jax.ShapeDty...  235 us

profile of v3, /device:TPU:1, one launch (start us, length us, event | category | flops | bytes accessed | tf_op | source)
XLA Modules:
  0.0 239.8 jit_solution(15993127020994670914)
XLA Ops:
  0.6 235.4 %moe_exchange.1 = (bf16[128,3584]{1,0:T(8,128)(2,1)}, bf16[576,128]{1,0:T(8,128)(2,1)}) custom-call(bf16[128,3584]{1,0:T(8,128)(2,1)} %tok.1, s32[8,128]{1,0:T(8,128)} %bitcast.7, bf16[8,128]{1,0:T(8,128)(2,1)} %bitcast.8, bf16[576,128]{1,0:T(8,128)(2,1)} %bitcast.6, s32[1,128]{1,0:T(1,128)} %bitcast.9, bf16[1,3584,1024]{2,1,0:T(8,128)(2,1)} %wg.1, ...), custom_call_target="tpu_custom_call" | custom-call | flops 28185722880 | bytes 22020096 | tf_op jit(solution)/shard_map/moe_exchange/pallas_call | solution.py:650
  236.0 2.2 copy.12
  238.2 1.6 copy.13

commit v4 on v3

--- a/solution.py
+++ b/solution.py
@@ -33,6 +33,8 @@
 PART_LAG = 5
 HOME_LAG = 7
 END_LAG = 8
+FLAT_FIRST = 2
+FLAT_LAST = 3
 STRIDE = 3
 BUILD = 128
 LAT_PAD = 640
@@ -237,19 +239,27 @@
 
     to_nodes(gate_out, gates.at[0], NODE_ROWS, sem_misc.at[0], sem_misc.at[1])
 
-    @pl.loop(0, TYPES)
-    def _(t):
-        there = (node, partner_at(t))
-        send(named, named_in.at[t], sem_named.at[0, t], sem_named.at[1, t], there)
-
-    @pl.loop(0, chunks)
-    def _(k):
-        there = (node, partner_at(k))
-        send(
-            tok.at[:, columns(k)], shared.at[k], sem_shared.at[0, k], sem_shared.at[1, k], there
-        )
-
-    gates[0, rows_at(node, NODE_ROWS), :] = gate_out[rows_at(node, NODE_ROWS), :]
+    flat_back = chunks - FLAT_LAST
+
+    def either(flat, ref, flat_rows, rows, sem):
+        @pl.when(flat)
+        def _():
+            wait_for(ref.at[pl.ds(0, flat_rows)], sem)
+
+        @pl.when(jnp.logical_not(flat))
+        def _():
+            wait_for(ref.at[pl.ds(0, rows)], sem)
+
+    def wait_node_rows(flat, ref, sem):
+        either(flat, ref, (NODES - 1) * NODE_ROWS, (NODES - 1) * PAIR_ROWS, sem)
+
+    def wait_slots(flat, ref, sem):
+        either(flat, ref, (LOCALS - 1) * CAP, REMOTE * CAP, sem)
+
+    def flat_node_send(k):
+        zs[k, 0:ROWS, :] = mm(choose[0], tok[:, columns(k)]).astype(BF16)
+        to_nodes(zs.at[k], passed.at[k], NODE_ROWS, sem_z.at[0, k], sem_z.at[1, k])
+        passed[k, rows_at(node, NODE_ROWS), :] = zs[k, rows_at(node, NODE_ROWS), :]
 
     def put_pair(slot, side, value):
         for n in range(NODES):
@@ -264,14 +274,15 @@
         t = lax.rem(k, TYPES)
         slot = lax.rem(k, ZS_SLOTS)
 
-        @pl.when(k < TYPES)
+        @pl.when(k < FLAT_FIRST + TYPES)
         def _():
             wait_for(named_in.at[t], sem_named.at[1, t])
             route(1 + t, named_in[t])
 
         @pl.when(k >= ZS_SLOTS)
         def _():
-            wait_for(zs.at[slot, pl.ds(0, (NODES - 1) * PAIR_ROWS)], sem_z.at[0, k - ZS_SLOTS])
+            old = k - ZS_SLOTS
+            wait_node_rows(old < FLAT_FIRST, zs.at[slot], sem_z.at[0, old])
 
         put_pair(slot, 0, mm(choose[0], tok[:, columns(k)]).astype(BF16))
         wait_for(shared.at[k], sem_shared.at[1, k])
@@ -324,7 +335,50 @@
                     q * BUILD : (q + 1) * BUILD, :
                 ]
 
-    node_send(0)
+    def build_flat_pick():
+        @pl.loop(0, SLOTS // BUILD)
+        def _(i):
+            slot = iota((BUILD, TOK), 0) + i * BUILD
+            lane = node * LOCALS + lax.div(slot, CAP)
+            spread = ones_where(iota((BUILD, TOK), 1) == lane).astype(BF16)
+            count_at = mm_nt(spread, counts[0])
+            wanted = (lax.rem(iota((BUILD, ROWS), 0) + i * BUILD, CAP) + 1).astype(F32)
+            hidden[rows_at(i, BUILD), 0:ROWS] = ones_where(count_at == wanted).astype(BF16)
+
+    def build_flat_combine():
+        @pl.loop(0, SLOTS // BUILD)
+        def _(i):
+            slot = iota((TOK, BUILD), 1) + i * BUILD
+            lane = node * LOCALS + lax.div(slot, CAP)
+            spread = ones_where(iota((TOK, BUILD), 0) == lane).astype(BF16)
+            count_at = mm(counts[0], spread)
+            gate_at = mm(gates[0], spread)
+            wanted = (lax.rem(iota((8, BUILD), 1) + i * BUILD, CAP)[0:1, :] + 1).astype(F32)
+            weight = jnp.where(count_at == wanted, gate_at, 0.0)
+            for q in range(ROWS // BUILD):
+                acc_up[rows_at(i, BUILD), q * BUILD : (q + 1) * BUILD] = weight[
+                    q * BUILD : (q + 1) * BUILD, :
+                ]
+
+    @pl.loop(0, FLAT_FIRST)
+    def _(k):
+        flat_node_send(k)
+
+    @pl.loop(0, TYPES)
+    def _(t):
+        there = (node, partner_at(t))
+        send(named, named_in.at[t], sem_named.at[0, t], sem_named.at[1, t], there)
+
+    @pl.loop(FLAT_FIRST, chunks)
+    def _(k):
+        there = (node, partner_at(k))
+        send(
+            tok.at[:, columns(k)], shared.at[k], sem_shared.at[0, k], sem_shared.at[1, k], there
+        )
+
+    gates[0, rows_at(node, NODE_ROWS), :] = gate_out[rows_at(node, NODE_ROWS), :]
+
+    node_send(FLAT_FIRST)
     wait_for(gates.at[0, pl.ds(0, (NODES - 1) * NODE_ROWS)], sem_misc.at[1])
 
     @pl.loop(0, TYPES)
@@ -333,8 +387,9 @@
         send(gates.at[0], gates.at[1 + t], sem_gates.at[0, t], sem_gates.at[1, t], there)
 
     count_rows(0)
-
-    @pl.loop(1, AHEAD)
+    build_flat_pick()
+
+    @pl.loop(FLAT_FIRST + 1, AHEAD)
     def _(k):
         node_send(k)
 
@@ -377,7 +432,8 @@
 
     def wait_group(k, cy):
         py, _ = partner_of(y, x, k)
-        missing = (cy == y).astype(jnp.int32) + (cy == py).astype(jnp.int32)
+        pairs = (k >= FLAT_FIRST) & (cy == py)
+        missing = (cy == y).astype(jnp.int32) + pairs.astype(jnp.int32)
         for skipped in range(3):
 
             @pl.when(missing == skipped)
@@ -411,11 +467,11 @@
             for copy in weights_in(k + 2):
                 copy.start()
 
-    def expert_rows(k):
+    def paired_rows(k):
         t = lax.rem(k, TYPES)
         slot = lax.rem(k, TX_SLOTS)
 
-        @pl.when(k < TYPES)
+        @pl.when(k < FLAT_FIRST + TYPES)
         def _():
             wait_for(gates.at[1 + t], sem_gates.at[1, t])
             count_rows(1 + t)
@@ -425,7 +481,8 @@
 
         @pl.when(k >= TX_SLOTS)
         def _():
-            wait_for(tx.at[slot, pl.ds(0, REMOTE * CAP)], sem_tx.at[k - TX_SLOTS])
+            old = k - TX_SLOTS
+            wait_slots(old < FLAT_FIRST, tx.at[slot], sem_tx.at[old])
 
         for side in range(2):
             arrived = get_pair(passed, k, side)
@@ -452,11 +509,32 @@
         rx[k, rows_at(local, CAP), :] = tx[slot, 0:CAP, :]
         rx[k, rows_at(py * SIDE + px, CAP), :] = tx[slot, HALF : HALF + CAP, :]
 
+    def flat_rows(k):
+        wait_for(passed.at[k, pl.ds(0, (NODES - 1) * NODE_ROWS)], sem_z.at[1, k])
+        tx[k] = mm(hidden[:, 0:ROWS], passed[k, 0:ROWS, :]).astype(BF16)
+
+        @pl.loop(1, LOCALS)
+        def _(d):
+            peer = local_peer(lax.rem(d * STRIDE, LOCALS))
+            send(
+                tx.at[k, rows_at(peer, CAP)],
+                rx.at[k, rows_at(local, CAP)],
+                sem_tx.at[k],
+                sem_rx.at[k, y],
+                (node, peer),
+            )
+
+        rx[k, rows_at(local, CAP), :] = tx[k, rows_at(local, CAP), :]
+
     @pl.loop(0, chunks - 1 + EXPERT_LAG)
     def _(k):
-        @pl.when(k < chunks)
-        def _():
-            expert_rows(k)
+        @pl.when(k < FLAT_FIRST)
+        def _():
+            flat_rows(k)
+
+        @pl.when((k >= FLAT_FIRST) & (k < chunks))
+        def _():
+            paired_rows(k)
 
         @pl.when(k + AHEAD < chunks)
         def _():
@@ -542,7 +620,8 @@
 
         @pl.when(k >= ZS_SLOTS)
         def _():
-            wait_for(zs.at[slot, pl.ds(0, (NODES - 1) * PAIR_ROWS)], sem_back.at[0, k - ZS_SLOTS])
+            old = k - ZS_SLOTS
+            wait_node_rows(old >= flat_back, zs.at[slot], sem_back.at[0, old])
 
         for side in range(2):
             weight = jnp.concatenate(
@@ -560,6 +639,25 @@
         to_nodes(zs.at[slot], back.at[k], PAIR_ROWS, sem_back.at[0, k], sem_back.at[1, k])
         back[k, rows_at(node, PAIR_ROWS), :] = zs[slot, rows_at(node, PAIR_ROWS), :]
 
+    flat_parts = [pl.ds(i * BUILD, BUILD) for i in range(SLOTS // BUILD)]
+
+    def flat_part(k):
+        slot = lax.rem(k, ZS_SLOTS)
+        wait_for(passed.at[k, pl.ds(0, (LOCALS - 1) * CAP)], sem_ret.at[1, k])
+        old = k - ZS_SLOTS
+        wait_node_rows(old >= flat_back, zs.at[slot], sem_back.at[0, old])
+        for q in range(ROWS // BUILD):
+            weight = jnp.concatenate(
+                [acc_up[part, pl.ds(q * BUILD, BUILD)] for part in flat_parts], axis=1
+            ).astype(BF16)
+            zs[slot, q * BUILD : (q + 1) * BUILD, :] = mm(weight, passed[k]).astype(BF16)
+        to_nodes(zs.at[slot], back.at[k], NODE_ROWS, sem_back.at[0, k], sem_back.at[1, k])
+        back[k, rows_at(node, NODE_ROWS), :] = zs[slot, rows_at(node, NODE_ROWS), :]
+
+    def flat_finish(k):
+        wait_for(back.at[k, pl.ds(0, (NODES - 1) * NODE_ROWS)], sem_back.at[1, k])
+        moe[:, columns(k)] = mm(choose_t[0], back[k, 0:ROWS, :]).astype(BF16)
+
     def to_partner(k):
         t = lax.rem(k, TYPES)
 
@@ -591,42 +689,67 @@
                 rows = rows_at(i, GROUP)
                 rx[k, rows, :] = mm(hidden[rows, :], wd_buf[slot]).astype(BF16)
 
-            @pl.loop(0, REMOTE)
-            def _(m):
-                j = 1 + lax.rem(m * STRIDE, COVER - 1)
-                send_back(k, j // SIDE, lax.rem(j, SIDE), m // (COVER - 1))
-
-            keep_back(k)
+            @pl.when(k < flat_back)
+            def _():
+                @pl.loop(0, REMOTE)
+                def _(m):
+                    j = 1 + lax.rem(m * STRIDE, COVER - 1)
+                    send_back(k, j // SIDE, lax.rem(j, SIDE), m // (COVER - 1))
+
+                keep_back(k)
+
+            @pl.when(k >= flat_back)
+            def _():
+                to_locals(rx.at[k], passed.at[k], CAP, sem_ret.at[0, k], sem_ret.at[1, k])
+                passed[k, rows_at(local, CAP), :] = rx[k, rows_at(local, CAP), :]
 
             @pl.when(k + 2 < chunks)
             def _():
                 down_in(k + 2).start()
 
-        @pl.when((k >= PART_LAG) & (k < chunks + PART_LAG))
+        @pl.when((k >= PART_LAG) & (k < flat_back + PART_LAG))
         def _():
             node_part(k - PART_LAG)
 
+        @pl.when((k >= flat_back + PART_LAG) & (k < chunks + PART_LAG))
+        def _():
+            flat_part(k - PART_LAG)
+
+        @pl.when(k == 10)
+        def _():
+            build_flat_combine()
+
         @pl.when(k == 9)
         def _():
             latent_third()
 
-        @pl.when((k >= HOME_LAG) & (k < chunks + HOME_LAG))
+        @pl.when((k >= HOME_LAG) & (k < flat_back + HOME_LAG))
         def _():
             to_partner(k - HOME_LAG)
 
-        @pl.when(k >= END_LAG)
+        @pl.when((k >= END_LAG) & (k < flat_back + END_LAG))
         def _():
             finish(k - END_LAG)
 
+        @pl.when(k >= flat_back + END_LAG)
+        def _():
+            flat_finish(k - END_LAG)
+
+    @pl.loop(FLAT_FIRST, chunks)
+    def _(k):
+        wait_for(shared.at[k], sem_shared.at[0, k])
+
     @pl.loop(0, chunks)
     def _(k):
-        wait_for(shared.at[k], sem_shared.at[0, k])
+        wait_slots(k >= flat_back, rx.at[k], sem_ret.at[0, k])
+
+    @pl.loop(0, flat_back)
+    def _(k):
         wait_for(shared.at[k], sem_home.at[0, k])
-        wait_for(rx.at[k, pl.ds(0, REMOTE * CAP)], sem_ret.at[0, k])
 
     @pl.loop(chunks - ZS_SLOTS, chunks)
     def _(k):
-        wait_for(zs.at[0, pl.ds(0, (NODES - 1) * PAIR_ROWS)], sem_back.at[0, k])
+        wait_node_rows(k >= flat_back, zs.at[0], sem_back.at[0, k])
 
     @pl.loop(0, TYPES)
     def _(t):

time: 240 us -> 225 us (0.938)
  Pallas kernels: 235 us -> 221 us
    pallas_call x1, Pallas kernels: 235 us -> 221 us  [per_device(): pl.pallas_call(functools.partial(kernel, chunks), out_shape=(jax.ShapeDty...]
where the time goes in v4:
time: 225 us
  Pallas kernels  221 us (98%)
  local copies, waits for them, and re-layouts  3.74 us (2%)
    pallas_call x1, Pallas kernels, per_device(): pl.pallas_call(functools.partial(kernel, chunks), out_shape=(jax.ShapeDty...  221 us

profile of v4, /device:TPU:1, one launch (start us, length us, event | category | flops | bytes accessed | tf_op | source)
XLA Modules:
  0.0 225.1 jit_solution(1882248888271598741)
XLA Ops:
  0.6 220.7 %moe_exchange.1 = (bf16[128,3584]{1,0:T(8,128)(2,1)}, bf16[576,128]{1,0:T(8,128)(2,1)}) custom-call(bf16[128,3584]{1,0:T(8,128)(2,1)} %tok.1, s32[8,128]{1,0:T(8,128)} %bitcast.7, bf16[8,128]{1,0:T(8,128)(2,1)} %bitcast.8, bf16[576,128]{1,0:T(8,128)(2,1)} %bitcast.6, s32[1,128]{1,0:T(1,128)} %bitcast.9, bf16[1,3584,1024]{2,1,0:T(8,128)(2,1)} %wg.1, ...), custom_call_target="tpu_custom_call" | custom-call | flops 28185722880 | bytes 22020096 | tf_op jit(solution)/shard_map/moe_exchange/pallas_call | solution.py:773
  221.3 2.2 copy.12
  223.5 1.6 copy.13

commit v5 on v4

--- a/solution.py
+++ b/solution.py
@@ -132,7 +132,7 @@
 
     def kind(k):
         t = lax.rem(k, TYPES)
-        return lax.rem(t, 2), t // 2
+        return t // 2, lax.rem(t, 2)
 
     def partner_of(py, px, t):
         along_x, way = kind(t)

time: 225 us -> 229 us (1.018)
  Pallas kernels: 221 us -> 224 us
    pallas_call x1, Pallas kernels: 221 us -> 224 us  [per_device(): pl.pallas_call(functools.partial(kernel, chunks), out_shape=(jax.ShapeDty...]
where the time goes in v5:
time: 229 us
  Pallas kernels  224 us (98%)
  local copies, waits for them, and re-layouts  3.74 us (2%)
    pallas_call x1, Pallas kernels, per_device(): pl.pallas_call(functools.partial(kernel, chunks), out_shape=(jax.ShapeDty...  224 us

profile of v5, /device:TPU:1, one launch (start us, length us, event | category | flops | bytes accessed | tf_op | source)
XLA Modules:
  0.0 228.8 jit_solution(5582787672377561272)
XLA Ops:
  0.6 224.4 %moe_exchange.1 = (bf16[128,3584]{1,0:T(8,128)(2,1)}, bf16[576,128]{1,0:T(8,128)(2,1)}) custom-call(bf16[128,3584]{1,0:T(8,128)(2,1)} %tok.1, s32[8,128]{1,0:T(8,128)} %bitcast.7, bf16[8,128]{1,0:T(8,128)(2,1)} %bitcast.8, bf16[576,128]{1,0:T(8,128)(2,1)} %bitcast.6, s32[1,128]{1,0:T(1,128)} %bitcast.9, bf16[1,3584,1024]{2,1,0:T(8,128)(2,1)} %wg.1, ...), custom_call_target="tpu_custom_call" | custom-call | flops 28185722880 | bytes 22020096 | tf_op jit(solution)/shard_map/moe_exchange/pallas_call | solution.py:773
  225.1 2.2 copy.12
  227.2 1.6 copy.13
